TPU v7x, 128 devices: a whole 4x4x4 slice. The times are simulated.
128 devices in a mesh: replica: 16 (over x_hi, z, core), group: 8 (over y, x_lo).
Axes of the slice: x: 4 (x_hi: 2, x_lo: 2; x = x_hi * 2 + x_lo), y: 4, z: 4, core: 2. Of those that a mesh axis runs over, the one named last changes fastest.
Arguments:
- tokens: bfloat16 [16384, 960], P(('replica', 'group')), may hold values from -6 to 6
- cotangent: bfloat16 [16384, 960], P(('replica', 'group')), may hold values from -6 to 6
- lengths: int32 [128, 3], P(('replica', 'group')), may hold values from 1 to 64, 128 in all within a row
- gain_attn: bfloat16 [2, 960], P(None, 'group'), may hold values from 0.5 to 1.5
- w_query: bfloat16 [2, 960, 960], P(None, 'group'), may hold values from -0.1875 to 0.1875
- w_key: bfloat16 [2, 960, 320], P(None, 'group'), may hold values from -0.1875 to 0.1875
- w_value: bfloat16 [2, 960, 320], P(None, 'group'), may hold values from -0.1875 to 0.1875
- w_out: bfloat16 [2, 960, 960], P(None, 'group'), may hold values from -1.5 to 1.5
- gain_mlp: bfloat16 [2, 960], P(None, 'group'), may hold values from 0.5 to 1.5
- w_gate: bfloat16 [2, 960, 2560], P(None, None, 'group'), may hold values from -0.1875 to 0.1875
- w_up: bfloat16 [2, 960, 2560], P(None, None, 'group'), may hold values from -0.1875 to 0.1875
- w_down: bfloat16 [2, 2560, 960], P(None, 'group'), may hold values from -0.125 to 0.125
Outputs:
- activations: bfloat16 [16384, 960], P(('replica', 'group'))
- grad_tokens: float32 [16384, 960], P(('replica', 'group'))
- grad_gain_attn: float32 [2, 960], P(None, 'group')
- grad_w_query: float32 [2, 960, 960], P(None, 'group')
- grad_w_key: float32 [2, 960, 320], P(None, 'group')
- grad_w_value: float32 [2, 960, 320], P(None, 'group')
- grad_w_out: float32 [2, 960, 960], P(None, 'group')
- grad_gain_mlp: float32 [2, 960], P(None, 'group')
- grad_w_gate: float32 [2, 960, 2560], P(None, None, 'group')
- grad_w_up: float32 [2, 960, 2560], P(None, None, 'group')
- grad_w_down: float32 [2, 2560, 960], P(None, 'group')
Inputs may be any that keep to these rules, and one draw needn't show every extreme that they name: Each row holds the lengths of 3 sequences that fill one device's 128 tokens in order; one of them is exactly 64 long.
All inputs are finite; a program needn't handle non-finite values.
Results may differ from a plain program's by a relative error of at most 0.03.
Values may be sent and summed in bfloat16 or wider, within the bound.
A program may use at most 192 MiB of HBM per device.

v0:
```python
import jax
import jax.numpy as jnp
from jax import lax
from jax.sharding import PartitionSpec as P

Q_HEADS = 15
KV_HEADS = 5
HEAD = 64
LAYERS = 2


norm_eps = 1e-05
rope_base = 100000.0
score_scale = 0.125
masked_value = -1e30


def rms_scale(stream, gain_vec):
    return (
        stream * lax.rsqrt(jnp.mean(stream * stream, axis=-1, keepdims=True) + norm_eps) * gain_vec
    )


def rope_tables(positions):
    steps_half = jnp.arange(HEAD // 2, dtype=jnp.float32)
    inverse = rope_base ** (-2.0 * steps_half / HEAD)
    angles = positions[:, None] * inverse[None, :]
    cosine = jnp.cos(angles)
    sine_table = jnp.sin(angles)
    return (
        jnp.concatenate([cosine, cosine], axis=1),
        jnp.concatenate([sine_table, sine_table], axis=1),
    )


def rotate(values, cosine, sine_table):
    amount = values.shape[0]
    shaped = values.reshape(amount, -1, HEAD)
    first_half = shaped[..., : HEAD // 2]
    second_half = shaped[..., HEAD // 2 :]
    turned = jnp.concatenate([-second_half, first_half], axis=-1)
    return (shaped * cosine[:, None, :] + turned * sine_table[:, None, :]).reshape(values.shape)


def rotate_back(grad_values, cosine, sine_table):
    amount = grad_values.shape[0]
    shaped = grad_values.reshape(amount, -1, HEAD)
    scaled = shaped * sine_table[:, None, :]
    turned = jnp.concatenate([scaled[..., HEAD // 2 :], -scaled[..., : HEAD // 2]], axis=-1)
    return (shaped * cosine[:, None, :] + turned).reshape(grad_values.shape)


def layout(seq_lengths, amount):
    finish = jnp.cumsum(seq_lengths)
    indices = jnp.arange(amount, dtype=jnp.int32)
    documents = jnp.sum((indices[:, None] >= finish[None, :]).astype(jnp.int32), axis=1)
    starts = finish - seq_lengths
    member = documents[:, None] == jnp.arange(seq_lengths.shape[0], dtype=jnp.int32)[None, :]
    begins = jnp.sum(jnp.where(member, starts[None, :], 0), axis=1)
    return (documents, indices - begins)


def times_transposed(left_side, right_side):
    return lax.dot_general(
        left_side, right_side, (((1,), (1,)), ((), ())), preferred_element_type=jnp.float32
    )


def transposed_times(left_side, right_side):
    return lax.dot_general(
        left_side, right_side, (((0,), (0,)), ((), ())), preferred_element_type=jnp.float32
    )


def split_queries(query_rows):
    own_rows = query_rows.shape[0]
    return query_rows.reshape(own_rows, KV_HEADS, Q_HEADS // KV_HEADS, HEAD).transpose(1, 2, 0, 3)


def split_keys(key_rows):
    return key_rows.reshape(key_rows.shape[0], KV_HEADS, HEAD).transpose(1, 0, 2)


def attention_forward(query_rot, key_rot, values, allowed):
    own_rows = query_rot.shape[0]

    def one_head(head_parts):
        query_head, key_head, value_head = head_parts
        scores = (
            jnp.einsum("gsd,td->gst", query_head, key_head, preferred_element_type=jnp.float32)
            * score_scale
        )
        scores = jnp.where(allowed[None], scores, masked_value)
        row_max = jnp.max(scores, axis=-1, keepdims=True)
        weights = jnp.exp(scores - row_max)
        row_total = jnp.sum(weights, axis=-1, keepdims=True)
        weights_low = (weights / row_total).astype(jnp.bfloat16)
        mixed_head = jnp.einsum(
            "gst,td->gsd", weights_low, value_head, preferred_element_type=jnp.float32
        )
        return (mixed_head, (row_max + jnp.log(row_total))[..., 0])

    mixed_heads, log_total = lax.map(
        one_head, (split_queries(query_rot), split_keys(key_rot), split_keys(values))
    )
    return (mixed_heads.transpose(2, 0, 1, 3).reshape(own_rows, Q_HEADS * HEAD), log_total)


def attention_backward(query_rot, key_rot, values, log_total, grad_mixed, allowed):
    own_rows = query_rot.shape[0]

    def one_head(head_parts):
        query_head, key_head, value_head, total_head, grad_head = head_parts
        scores = (
            jnp.einsum("gsd,td->gst", query_head, key_head, preferred_element_type=jnp.float32)
            * score_scale
        )
        scores = jnp.where(allowed[None], scores, masked_value)
        weights_soft = jnp.exp(scores - total_head[..., None])
        grad_probs = jnp.einsum(
            "gsd,td->gst", grad_head, value_head, preferred_element_type=jnp.float32
        )
        row_inner = jnp.sum(weights_soft * grad_probs, axis=-1, keepdims=True)
        grad_scores = (weights_soft * (grad_probs - row_inner)).astype(jnp.bfloat16)
        grad_query = (
            jnp.einsum("gst,td->gsd", grad_scores, key_head, preferred_element_type=jnp.float32)
            * score_scale
        )
        grad_key = (
            jnp.einsum("gst,gsd->td", grad_scores, query_head, preferred_element_type=jnp.float32)
            * score_scale
        )
        grad_value = jnp.einsum(
            "gst,gsd->td",
            weights_soft.astype(jnp.bfloat16),
            grad_head,
            preferred_element_type=jnp.float32,
        )
        return (grad_query, grad_key, grad_value)

    grad_query, grad_key, grad_value = lax.map(
        one_head,
        (
            split_queries(query_rot),
            split_keys(key_rot),
            split_keys(values),
            log_total,
            split_queries(grad_mixed),
        ),
    )
    return (
        grad_query.transpose(2, 0, 1, 3).reshape(own_rows, Q_HEADS * HEAD),
        grad_key.transpose(1, 0, 2).reshape(own_rows, KV_HEADS * HEAD),
        grad_value.transpose(1, 0, 2).reshape(own_rows, KV_HEADS * HEAD),
    )


def shards(
    tokens,
    cotangent,
    lengths,
    gain_attn,
    w_query,
    w_key,
    w_value,
    w_out,
    gain_mlp,
    w_gate,
    w_up,
    w_down,
):
    own_rows = tokens.shape[0]
    doc_own, pos_own = layout(lengths[0], own_rows)
    cosine, sine_table = rope_tables(pos_own.astype(jnp.float32))
    row_index = jnp.arange(own_rows, dtype=jnp.int32)
    allowed = (doc_own[:, None] == doc_own[None, :]) & (row_index[None, :] <= row_index[:, None])

    def fetch_attention(layer_index):
        return (
            lax.all_gather(gain_attn[layer_index], "group", axis=0, tiled=True),
            lax.all_gather(w_query[layer_index], "group", axis=0, tiled=True),
            lax.all_gather(w_key[layer_index], "group", axis=0, tiled=True),
            lax.all_gather(w_value[layer_index], "group", axis=0, tiled=True),
            lax.all_gather(w_out[layer_index], "group", axis=0, tiled=True),
            lax.all_gather(gain_mlp[layer_index], "group", axis=0, tiled=True),
        )

    def fetch_mlp(layer_index):
        return (
            lax.all_gather(w_gate[layer_index], "group", axis=1, tiled=True),
            lax.all_gather(w_up[layer_index], "group", axis=1, tiled=True),
            lax.all_gather(w_down[layer_index], "group", axis=0, tiled=True),
        )

    stream = tokens.astype(jnp.float32)
    saved_layers = []
    for layer_index in range(LAYERS):
        gain_one, query_w, key_w, value_w, out_w, gain_two = fetch_attention(layer_index)
        normed = rms_scale(stream, gain_one.astype(jnp.float32)).astype(jnp.bfloat16)
        query_proj = jnp.dot(normed, query_w, preferred_element_type=jnp.float32)
        key_proj = jnp.dot(normed, key_w, preferred_element_type=jnp.float32)
        values = jnp.dot(normed, value_w, preferred_element_type=jnp.float32).astype(jnp.bfloat16)
        query_rot = rotate(query_proj, cosine, sine_table).astype(jnp.bfloat16)
        key_rot = rotate(key_proj, cosine, sine_table).astype(jnp.bfloat16)
        mixed, log_total = attention_forward(query_rot, key_rot, values, allowed)
        mixed_low = mixed.astype(jnp.bfloat16)
        hidden = stream + jnp.dot(mixed_low, out_w, preferred_element_type=jnp.float32)
        normed_two = rms_scale(hidden, gain_two.astype(jnp.float32)).astype(jnp.bfloat16)
        gate_w, up_w, down_w = fetch_mlp(layer_index)
        mlp_in = normed_two
        gate_pre = jnp.dot(mlp_in, gate_w, preferred_element_type=jnp.float32)
        up_pre = jnp.dot(mlp_in, up_w, preferred_element_type=jnp.float32)
        active = (gate_pre * jax.nn.sigmoid(gate_pre) * up_pre).astype(jnp.bfloat16)
        result = hidden + jnp.dot(active, down_w, preferred_element_type=jnp.float32)
        saved_layers.append(
            (
                stream,
                hidden,
                normed,
                query_rot,
                key_rot,
                values,
                log_total,
                mixed_low,
                mlp_in,
                gate_pre,
                up_pre,
            )
        )
        stream = result
    grad_stream = cotangent.astype(jnp.float32)
    collected = [None] * LAYERS
    for layer_index in reversed(range(LAYERS)):
        (
            layer_in,
            hidden,
            normed,
            query_rot,
            key_rot,
            values,
            log_total,
            mixed_low,
            mlp_in,
            gate_pre,
            up_pre,
        ) = saved_layers[layer_index]
        gain_one, query_w, key_w, value_w, out_w, gain_two = fetch_attention(layer_index)
        grad_low = grad_stream.astype(jnp.bfloat16)
        gate_sigmoid = jax.nn.sigmoid(gate_pre)
        active = (gate_pre * gate_sigmoid * up_pre).astype(jnp.bfloat16)
        gate_w, up_w, down_w = fetch_mlp(layer_index)
        grad_active = times_transposed(grad_low, down_w)
        grad_gate = (
            grad_active * up_pre * gate_sigmoid * (1.0 + gate_pre * (1.0 - gate_sigmoid))
        ).astype(jnp.bfloat16)
        grad_up = (grad_active * gate_pre * gate_sigmoid).astype(jnp.bfloat16)
        grad_input = times_transposed(grad_gate, gate_w) + times_transposed(grad_up, up_w)
        grad_gate_w = transposed_times(mlp_in, grad_gate)
        grad_up_w = transposed_times(mlp_in, grad_up)
        grad_down_w = transposed_times(active, grad_low)
        grad_gate_w, grad_up_w, grad_down_w = (
            lax.psum_scatter(
                grad_gate_w.astype(jnp.bfloat16), "group", scatter_dimension=1, tiled=True
            ).astype(jnp.float32),
            lax.psum_scatter(
                grad_up_w.astype(jnp.bfloat16), "group", scatter_dimension=1, tiled=True
            ).astype(jnp.float32),
            lax.psum_scatter(
                grad_down_w.astype(jnp.bfloat16), "group", scatter_dimension=0, tiled=True
            ).astype(jnp.float32),
        )
        norm_value, norm_back = jax.vjp(rms_scale, hidden, gain_two.astype(jnp.float32))
        grad_hidden_norm, grad_gain_two = norm_back(grad_input)
        grad_hidden = grad_stream + grad_hidden_norm
        grad_hidden_low = grad_hidden.astype(jnp.bfloat16)
        grad_mixed = times_transposed(grad_hidden_low, out_w).astype(jnp.bfloat16)
        grad_out_w = transposed_times(mixed_low, grad_hidden_low)
        grad_query_rot, grad_key_rot, grad_value_sum = attention_backward(
            query_rot, key_rot, values, log_total, grad_mixed, allowed
        )
        grad_query = rotate_back(grad_query_rot, cosine, sine_table).astype(jnp.bfloat16)
        grad_keys = rotate_back(grad_key_rot, cosine, sine_table).astype(jnp.bfloat16)
        grad_values = grad_value_sum.astype(jnp.bfloat16)
        grad_normed = (
            times_transposed(grad_query, query_w)
            + times_transposed(grad_keys, key_w)
            + times_transposed(grad_values, value_w)
        )
        grad_query_w = transposed_times(normed, grad_query)
        grad_key_w = transposed_times(normed, grad_keys)
        grad_value_w = transposed_times(normed, grad_values)
        norm_first, back_first = jax.vjp(rms_scale, layer_in, gain_one.astype(jnp.float32))
        grad_stream_norm, grad_gain_one = back_first(grad_normed)
        grad_stream = grad_hidden + grad_stream_norm
        grad_gain_one, grad_query_w, grad_key_w, grad_value_w, grad_out_w, grad_gain_two = (
            lax.psum_scatter(
                grad_gain_one.astype(jnp.bfloat16), "group", scatter_dimension=0, tiled=True
            ).astype(jnp.float32),
            lax.psum_scatter(
                grad_query_w.astype(jnp.bfloat16), "group", scatter_dimension=0, tiled=True
            ).astype(jnp.float32),
            lax.psum_scatter(
                grad_key_w.astype(jnp.bfloat16), "group", scatter_dimension=0, tiled=True
            ).astype(jnp.float32),
            lax.psum_scatter(
                grad_value_w.astype(jnp.bfloat16), "group", scatter_dimension=0, tiled=True
            ).astype(jnp.float32),
            lax.psum_scatter(
                grad_out_w.astype(jnp.bfloat16), "group", scatter_dimension=0, tiled=True
            ).astype(jnp.float32),
            lax.psum_scatter(
                grad_gain_two.astype(jnp.bfloat16), "group", scatter_dimension=0, tiled=True
            ).astype(jnp.float32),
        )
        layer_set = (
            grad_gain_one,
            grad_query_w,
            grad_key_w,
            grad_value_w,
            grad_out_w,
            grad_gain_two,
            grad_gate_w,
            grad_up_w,
            grad_down_w,
        )
        collected[layer_index] = layer_set
    stacked = [
        jnp.stack([collected[layer_index][kind_index] for layer_index in range(LAYERS)])
        for kind_index in range(9)
    ]
    stacked = (
        lax.psum(stacked[0].astype(jnp.bfloat16), "replica").astype(jnp.float32),
        lax.psum(stacked[1].astype(jnp.bfloat16), "replica").astype(jnp.float32),
        lax.psum(stacked[2].astype(jnp.bfloat16), "replica").astype(jnp.float32),
        lax.psum(stacked[3].astype(jnp.bfloat16), "replica").astype(jnp.float32),
        lax.psum(stacked[4].astype(jnp.bfloat16), "replica").astype(jnp.float32),
        lax.psum(stacked[5].astype(jnp.bfloat16), "replica").astype(jnp.float32),
        lax.psum(stacked[6].astype(jnp.bfloat16), "replica").astype(jnp.float32),
        lax.psum(stacked[7].astype(jnp.bfloat16), "replica").astype(jnp.float32),
        lax.psum(stacked[8].astype(jnp.bfloat16), "replica").astype(jnp.float32),
    )
    return (
        stream.astype(jnp.bfloat16),
        grad_stream,
        stacked[0],
        stacked[1],
        stacked[2],
        stacked[3],
        stacked[4],
        stacked[5],
        stacked[6],
        stacked[7],
        stacked[8],
    )


def solution(mesh):
    in_specs = (
        P(("replica", "group"), None),
        P(("replica", "group"), None),
        P(("replica", "group"), None),
        P(None, "group"),
        P(None, "group", None),
        P(None, "group", None),
        P(None, "group", None),
        P(None, "group", None),
        P(None, "group"),
        P(None, None, "group"),
        P(None, None, "group"),
        P(None, "group", None),
    )
    out_specs = (
        P(("replica", "group"), None),
        P(("replica", "group"), None),
        P(None, "group"),
        P(None, "group", None),
        P(None, "group", None),
        P(None, "group", None),
        P(None, "group", None),
        P(None, "group"),
        P(None, None, "group"),
        P(None, None, "group"),
        P(None, "group", None),
    )
    return jax.shard_map(shards, mesh=mesh, in_specs=in_specs, out_specs=out_specs, check_vma=False)
```

profile of v0, /device:TPU:1, one launch (start us, length us, event | category | flops | bytes accessed | tf_op | source)
XLA Modules:
  0.0 2273.5 jit_solution(3937638812315627804)
XLA Ops:
  21.2 18.0 all-reduce.15
  39.6 50.0 %all-gather.2 = bf16[1,960,320]{2,0,1:T(2,128)(2,1)S(1)} all-gather(bf16[1,120,320]{2,0,1:T(2,128)(2,1)S(1)} %copy.91), channel_id=4, replica_groups=mesh['replica'=16,'group'=8] {'group'}, dimensions={1}, use_global_device_ids=true | all-gather | bytes 691200 | tf_op jit(solution)/shard_map/all_gather | solution.py:182
  94.5 58.0 %all-gather.3 = bf16[1,960,320]{2,0,1:T(2,128)(2,1)S(1)} all-gather(bf16[1,120,320]{2,0,1:T(2,128)(2,1)S(1)} %copy.92), channel_id=5, replica_groups=mesh['replica'=16,'group'=8] {'group'}, dimensions={1}, use_global_device_ids=true | all-gather | bytes 691200 | tf_op jit(solution)/shard_map/all_gather | solution.py:183
  157.7 44.9 %all-gather.11 = bf16[1,960,320]{2,0,1:T(2,128)(2,1)S(1)} all-gather(bf16[1,120,320]{2,0,1:T(2,128)(2,1)S(1)} %copy.93), channel_id=13, replica_groups=mesh['replica'=16,'group'=8] {'group'}, dimensions={1}, use_global_device_ids=true | all-gather | bytes 691200 | tf_op jit(solution)/shard_map/all_gather | solution.py:182
  205.2 58.1 %all-gather.12 = bf16[1,960,320]{2,0,1:T(2,128)(2,1)S(1)} all-gather(bf16[1,120,320]{2,0,1:T(2,128)(2,1)S(1)} %copy.94), channel_id=14, replica_groups=mesh['replica'=16,'group'=8] {'group'}, dimensions={1}, use_global_device_ids=true | all-gather | bytes 691200 | tf_op jit(solution)/shard_map/all_gather | solution.py:183
  276.4 42.2 %all-gather.33.cloned.1.call-done = bf16[1,960,2560]{1,2,0:T(8,128)(2,1)} async-done(((bf16[1,960,320]{1,2,0:T(8,128)(2,1)}), bf16[1,960,2560]{1,2,0:T(8,128)(2,1)}) %all-gather.33.cloned.1.call-update) | async-done | bytes 4915216 | tf_op jit(solution)/shard_map/all_gather | solution.py:190
  324.1 106.9 %all-gather.35.cloned.1.call-done = bf16[1,960,2560]{1,2,0:T(8,128)(2,1)} async-done(((bf16[1,960,320]{1,2,0:T(8,128)(2,1)}), bf16[1,960,2560]{1,2,0:T(8,128)(2,1)}) %all-gather.35.cloned.1.call-update) | async-done | bytes 4915216 | tf_op jit(solution)/shard_map/all_gather | solution.py:191
  431.0 6.1 multiply_convert_fusion.7
  437.0 105.8 %all-gather.37.cloned.1.call-done = bf16[1,2560,960]{2,1,0:T(8,128)(2,1)} async-done(((bf16[1,320,960]{2,1,0:T(8,128)(2,1)}), bf16[1,2560,960]{2,1,0:T(8,128)(2,1)}) %all-gather.37.cloned.1.call-update) | async-done | bytes 4915216 | tf_op jit(solution)/shard_map/all_gather | solution.py:192
  547.9 47.1 %all-gather.39.cloned.1.call-done = bf16[1,960,960]{2,1,0:T(8,128)(2,1)} async-done(((bf16[1,120,960]{2,1,0:T(8,128)(2,1)}), bf16[1,960,960]{2,1,0:T(8,128)(2,1)}) %all-gather.39.cloned.1.call-update) | async-done | bytes 1843216 | tf_op jit(solution)/shard_map/all_gather | solution.py:181
  602.2 43.9 %all-gather.41.cloned.1.call-done = bf16[1,960,960]{2,1,0:T(8,128)(2,1)} async-done(((bf16[1,120,960]{2,1,0:T(8,128)(2,1)}), bf16[1,960,960]{2,1,0:T(8,128)(2,1)}) %all-gather.41.cloned.1.call-update) | async-done | bytes 1843216 | tf_op jit(solution)/shard_map/all_gather | solution.py:184
  649.3 108.3 %all-gather.45.cloned.1.call-done = bf16[1,960,2560]{1,2,0:T(8,128)(2,1)} async-done(((bf16[1,960,320]{1,2,0:T(8,128)(2,1)}), bf16[1,960,2560]{1,2,0:T(8,128)(2,1)}) %all-gather.45.cloned.1.call-update) | async-done | bytes 4915216 | tf_op jit(solution)/shard_map/all_gather | solution.py:191
  757.6 5.5 fusion.106
  763.1 106.5 %all-gather.47.cloned.1.call-done = bf16[1,2560,960]{2,1,0:T(8,128)(2,1)} async-done(((bf16[1,320,960]{2,1,0:T(8,128)(2,1)}), bf16[1,2560,960]{2,1,0:T(8,128)(2,1)}) %all-gather.47.cloned.1.call-update) | async-done | bytes 4915216 | tf_op jit(solution)/shard_map/all_gather | solution.py:192
  875.1 107.0 %all-gather.43.cloned.1.call-done = bf16[1,960,2560]{1,2,0:T(8,128)(2,1)} async-done(((bf16[1,960,320]{1,2,0:T(8,128)(2,1)}), bf16[1,960,2560]{1,2,0:T(8,128)(2,1)}) %all-gather.43.cloned.1.call-update) | async-done | bytes 4915216 | tf_op jit(solution)/shard_map/all_gather | solution.py:190
  982.1 6.3 multiply_convert_fusion.5
  999.3 31.9 %while.58 = (s32[]{:T(128)}, f32[5,3,128,64]{2,3,1,0:T(8,128)}, f32[5,128,64]{1,2,0:T(8,128)}, bf16[5,128,64]{1,2,0:T(8,128)(2,1)S(1)}, bf16[5,3,128,64]{2,3,1,0...) while((s32[]{:T(128)}, f32[5,3,128,64]{2,3,1,0:T(8,128)}, ...), condition=%wide.region_18.19_spmd.clone, body=%wide.region_16.18_spmd.clone.sunk | while | flops 31981184 | bytes 1930353 | solution.py:141
  1050.1 28.4 %while.59 = (s32[]{:T(128)}, f32[5,3,128,64]{2,3,1,0:T(8,128)S(1)}, f32[5,128,64]{1,2,0:T(8,128)}, bf16[5,128,64]{1,2,0:T(8,128)(2,1)S(1)}, bf16[5,3,128,64]{2,3...) while((s32[]{:T(128)}, f32[5,3,128,64]{2,3,1,0:T(8,128)S(1)}, ...), condition=%wide.region_23.24_spmd.clone, body=%wide.region_21.23_spmd.clone.sunk | while | flops 31981184 | bytes 1930353 | solution.py:141
  1124.8 85.0 %all-reduce.22.cloned.1.call-done = (bf16[960,320]{0,1:T(8,128)(2,1)}, bf16[960,320]{0,1:T(8,128)(2,1)}, bf16[960,320]{0,1:T(8,128)(2,1)}, bf16[960,320]{0,1:T(8,128)(2,1)}) async-done(((bf16[960,320]{0,1:T(8,128)(2,1)}, bf16[960,320]{0,1:T(8,128)(2,1)}, bf16[960,320]{0,1:T(8,128)(2,1)}, bf16[960,320]{0,1:T(8,128)(2,1)}), (bf16[960,320]{0,1:T(8,128)(2,1)}, bf16[960,320]{0,1:T(8,128)(2,1)}, ...) | async-done | bytes 2457616
  1213.4 48.8 %reduce-scatter.21.cloned.1.call-done = bf16[120,960]{1,0:T(8,128)(2,1)} async-done(((bf16[960,960]{1,0:T(8,128)(2,1)}), bf16[120,960]{1,0:T(8,128)(2,1)}) %reduce-scatter.21.cloned.1.call-update) | async-done | bytes 230416 | tf_op jit(solution)/shard_map/reduce_scatter | solution.py:308
  1262.3 51.9 %reduce-scatter.19.cloned.1.call-done = bf16[120,960]{1,0:T(8,128)(2,1)} async-done(((bf16[960,960]{1,0:T(8,128)(2,1)}), bf16[120,960]{1,0:T(8,128)(2,1)}) %reduce-scatter.19.cloned.1.call-update) | async-done | bytes 230416 | tf_op jit(solution)/shard_map/reduce_scatter | solution.py:308
  1316.0 50.3 %reduce-scatter.17.cloned.1.call-done = bf16[120,960]{1,0:T(8,128)(2,1)} async-done(((bf16[960,960]{1,0:T(8,128)(2,1)}), bf16[120,960]{1,0:T(8,128)(2,1)}) %reduce-scatter.17.cloned.1.call-update) | async-done | bytes 230416 | tf_op jit(solution)/shard_map/reduce_scatter | solution.py:299
  1366.3 52.3 %reduce-scatter.15.cloned.1.call-done = bf16[120,960]{1,0:T(8,128)(2,1)} async-done(((bf16[960,960]{1,0:T(8,128)(2,1)}), bf16[120,960]{1,0:T(8,128)(2,1)}) %reduce-scatter.15.cloned.1.call-update) | async-done | bytes 230416 | tf_op jit(solution)/shard_map/reduce_scatter | solution.py:299
  1420.5 110.3 %reduce-scatter.31.cloned.1.call-done = bf16[320,960]{1,0:T(8,128)(2,1)} async-done(((bf16[2560,960]{1,0:T(8,128)(2,1)}), bf16[320,960]{1,0:T(8,128)(2,1)}) %reduce-scatter.31.cloned.1.call-update) | async-done | bytes 614416 | tf_op jit(solution)/shard_map/reduce_scatter | solution.py:268
  1530.7 113.2 %reduce-scatter.33.cloned.1.call-done = bf16[320,960]{1,0:T(8,128)(2,1)} async-done(((bf16[2560,960]{1,0:T(8,128)(2,1)}), bf16[320,960]{1,0:T(8,128)(2,1)}) %reduce-scatter.33.cloned.1.call-update) | async-done | bytes 614416 | tf_op jit(solution)/shard_map/reduce_scatter | solution.py:268
  1646.4 110.8 %reduce-scatter.29.cloned.1.call-done = bf16[960,320]{0,1:T(8,128)(2,1)} async-done(((bf16[960,2560]{0,1:T(8,128)(2,1)}), bf16[960,320]{0,1:T(8,128)(2,1)}) %reduce-scatter.29.cloned.1.call-update) | async-done | bytes 614416 | tf_op jit(solution)/shard_map/reduce_scatter | solution.py:265
  1757.2 113.4 %reduce-scatter.27.cloned.1.call-done = bf16[960,320]{0,1:T(8,128)(2,1)} async-done(((bf16[960,2560]{0,1:T(8,128)(2,1)}), bf16[960,320]{0,1:T(8,128)(2,1)}) %reduce-scatter.27.cloned.1.call-update) | async-done | bytes 614416 | tf_op jit(solution)/shard_map/reduce_scatter | solution.py:265
  1873.1 110.8 %reduce-scatter.25.cloned.1.call-done = bf16[960,320]{0,1:T(8,128)(2,1)} async-done(((bf16[960,2560]{0,1:T(8,128)(2,1)}), bf16[960,320]{0,1:T(8,128)(2,1)}) %reduce-scatter.25.cloned.1.call-update) | async-done | bytes 614416 | tf_op jit(solution)/shard_map/reduce_scatter | solution.py:262
  1983.8 113.4 %reduce-scatter.23.cloned.1.call-done = bf16[960,320]{0,1:T(8,128)(2,1)} async-done(((bf16[960,2560]{0,1:T(8,128)(2,1)}), bf16[960,320]{0,1:T(8,128)(2,1)}) %reduce-scatter.23.cloned.1.call-update) | async-done | bytes 614416 | tf_op jit(solution)/shard_map/reduce_scatter | solution.py:262
  2103.2 14.9 all-reduce.14
  2118.3 37.0 %all-reduce.12 = (bf16[2,120]{1,0:T(2,128)(2,1)S(1)}, bf16[2,120]{1,0:T(2,128)(2,1)S(1)}) all-reduce(bf16[2,120]{1,0:T(2,128)(2,1)S(1)} %pad_maximum_fusion.11, bf16[2,120]{1,0:T(2,128)(2,1)S(1)} %pad_maximum_fusion.12), channel_id=1, replica_groups=mesh['replica'=16,'group'=8] {'replica'}, use_global_device_ids=true, to_apply=%region_29.30 | all-reduce | flops 480 | bytes 1920 | tf_op jit(solution)/shard_map/psum | solution.py:332
  2162.4 93.6 %all-reduce.20.cloned.1.call-done = (bf16[2,120,960]{2,1,0:T(8,128)(2,1)}, bf16[2,120,320]{1,2,0:T(8,128)(2,1)}, bf16[2,120,320]{1,2,0:T(8,128)(2,1)}, bf16[2,12...) async-done(((bf16[2,120,960]{2,1,0:T(8,128)(2,1)}, bf16[2,120,320]{1,2,0:T(8,128)(2,1)}, ...) | async-done | bytes 4915216 | tf_op jit(solution)/shard_map/psum | solution.py:333
  (501 shorter events, 241.2 us)
Async XLA Ops:
  7.2 259.6 %all-gather.29.cloned.1.call-start = ((), (), s32[]{:S(2)}) async-start(), calls=%async_computation.20 | async-start | bytes 2211840 | tf_op jit(solution)/shard_map/all_gather | solution.py:181
  9.2 264.3 %all-gather.31.cloned.1.call-start = ((), (), s32[]{:S(2)}) async-start(), calls=%async_computation.21 | async-start | bytes 2211840 | tf_op jit(solution)/shard_map/all_gather | solution.py:184
  11.2 307.4 %all-gather.33.cloned.1.call-start = ((), (), s32[]{:S(2)}) async-start(), calls=%async_computation.22 | async-start | bytes 5898240 | tf_op jit(solution)/shard_map/all_gather | solution.py:190
  12.4 418.5 %all-gather.35.cloned.1.call-start = ((), (), s32[]{:S(2)}) async-start(), calls=%async_computation.23 | async-start | bytes 5898240 | tf_op jit(solution)/shard_map/all_gather | solution.py:191
  14.1 528.7 %all-gather.37.cloned.1.call-start = ((), (), s32[]{:S(2)}) async-start(), calls=%async_computation.24 | async-start | bytes 5898240 | tf_op jit(solution)/shard_map/all_gather | solution.py:192
  15.4 579.5 %all-gather.39.cloned.1.call-start = ((), (), s32[]{:S(2)}) async-start(), calls=%async_computation.25 | async-start | bytes 2211840 | tf_op jit(solution)/shard_map/all_gather | solution.py:181
  16.0 630.1 %all-gather.41.cloned.1.call-start = ((), (), s32[]{:S(2)}) async-start(), calls=%async_computation.26 | async-start | bytes 2211840 | tf_op jit(solution)/shard_map/all_gather | solution.py:184
  16.7 740.9 %all-gather.45.cloned.1.call-start = ((), (), s32[]{:S(2)}) async-start(), calls=%async_computation.28 | async-start | bytes 5898240 | tf_op jit(solution)/shard_map/all_gather | solution.py:191
  17.5 852.1 %all-gather.47.cloned.1.call-start = ((), (), s32[]{:S(2)}) async-start(), calls=%async_computation.29 | async-start | bytes 5898240 | tf_op jit(solution)/shard_map/all_gather | solution.py:192
  18.2 963.9 %all-gather.43.cloned.1.call-start = ((), (), s32[]{:S(2)}) async-start(), calls=%async_computation.27 | async-start | bytes 5898240 | tf_op jit(solution)/shard_map/all_gather | solution.py:190
  18.8 1191.0 %all-reduce.22.cloned.1.call-start = ((), (), s32[]{:S(2)}) async-start(), calls=%async_computation.31 | async-start | bytes 5242880
  18.9 138.6 %copy-start.14 = (bf16[5,3,128,64]{2,3,1,0:T(8,128)(2,1)}, bf16[5,3,128,64]{2,3,1,0:T(8,128)(2,1)S(1)}, u32[]{:S(2)}) copy-start(bf16[5,3,128,64]{2,3,1,0:T(8,128)(2,1)S(1)} %fusion.243) | copy-start | bytes 737284
  19.0 247.7 %copy-start.35 = (bf16[5,128,64]{1,2,0:T(8,128)(2,1)}, bf16[5,128,64]{1,2,0:T(8,128)(2,1)S(1)}, u32[]{:S(2)}) copy-start(bf16[5,128,64]{1,2,0:T(8,128)(2,1)S(1)} %fusion.245) | copy-start | bytes 245764
  39.3 52.7 %copy-start.69 = (f32[128]{0:T(128)}, f32[128]{0:T(128)S(1)}, u32[]{:S(2)}) copy-start(f32[128]{0:T(128)S(1)} %fusion.201) | copy-start | bytes 1540
  92.0 63.9 %copy-start.24 = (bf16[1,960,320]{1,2,0:T(8,128)(2,1)}, bf16[1,960,320]{1,2,0:T(8,128)(2,1)S(1)}, u32[]{:S(2)}) copy-start(bf16[1,960,320]{1,2,0:T(8,128)(2,1)S(1)} %copy.68) | copy-start | bytes 1843204
  205.2 61.5 %copy-start.51 = (f32[128,5,32]{0,2,1:T(8,128)S(1)}, f32[128,5,32]{0,2,1:T(8,128)}, u32[]{:S(2)}) copy-start(f32[128,5,32]{0,2,1:T(8,128)} %get-tuple-element.427) | copy-start | bytes 245764
  205.2 61.5 %copy-start.52 = (f32[128,5,32]{0,2,1:T(8,128)S(1)}, f32[128,5,32]{0,2,1:T(8,128)}, u32[]{:S(2)}) copy-start(f32[128,5,32]{0,2,1:T(8,128)} %get-tuple-element.428) | copy-start | bytes 245764
  273.5 50.6 %copy-start.12 = (bf16[5,3,128,64]{2,3,1,0:T(8,128)(2,1)}, bf16[5,3,128,64]{2,3,1,0:T(8,128)(2,1)S(1)}, u32[]{:S(2)}) copy-start(bf16[5,3,128,64]{2,3,1,0:T(8,128)(2,1)S(1)} %get-tuple-element.871) | copy-start | bytes 737284
  649.3 332.8 %copy-start.6 = (bf16[128,960]{0,1:T(8,128)(2,1)}, bf16[128,960]{0,1:T(8,128)(2,1)S(1)}, u32[]{:S(2)}) copy-start(bf16[128,960]{0,1:T(8,128)(2,1)S(1)} %multiply_convert_fusion.8) | copy-start | bytes 737284
  757.6 112.0 %copy-start.29 = (bf16[128,960]{0,1:T(8,128)(2,1)S(1)}, bf16[128,960]{0,1:T(8,128)(2,1)}, u32[]{:S(2)}) copy-start(bf16[128,960]{0,1:T(8,128)(2,1)} %param.21) | copy-start | bytes 737284
  1083.2 179.1 %reduce-scatter.21.cloned.1.call-start = ((), (), s32[]{:S(2)}) async-start(), calls=%async_computation.13 | async-start | bytes 2211840 | tf_op jit(solution)/shard_map/reduce_scatter | solution.py:308
  1086.1 228.0 %reduce-scatter.19.cloned.1.call-start = ((), (), s32[]{:S(2)}) async-start(), calls=%async_computation.12 | async-start | bytes 2211840 | tf_op jit(solution)/shard_map/reduce_scatter | solution.py:308
  1089.2 277.1 %reduce-scatter.17.cloned.1.call-start = ((), (), s32[]{:S(2)}) async-start(), calls=%async_computation.11 | async-start | bytes 2211840 | tf_op jit(solution)/shard_map/reduce_scatter | solution.py:299
  1091.6 327.0 %reduce-scatter.15.cloned.1.call-start = ((), (), s32[]{:S(2)}) async-start(), calls=%async_computation.10 | async-start | bytes 2211840 | tf_op jit(solution)/shard_map/reduce_scatter | solution.py:299
  1093.9 436.8 %reduce-scatter.31.cloned.1.call-start = ((), (), s32[]{:S(2)}) async-start(), calls=%async_computation.18 | async-start | bytes 5898240 | tf_op jit(solution)/shard_map/reduce_scatter | solution.py:268
  1097.9 546.0 %reduce-scatter.33.cloned.1.call-start = ((), (), s32[]{:S(2)}) async-start(), calls=%async_computation.19 | async-start | bytes 5898240 | tf_op jit(solution)/shard_map/reduce_scatter | solution.py:268
  1103.0 654.2 %reduce-scatter.29.cloned.1.call-start = ((), (), s32[]{:S(2)}) async-start(), calls=%async_computation.17 | async-start | bytes 5898240 | tf_op jit(solution)/shard_map/reduce_scatter | solution.py:265
  1108.8 761.8 %reduce-scatter.27.cloned.1.call-start = ((), (), s32[]{:S(2)}) async-start(), calls=%async_computation.16 | async-start | bytes 5898240 | tf_op jit(solution)/shard_map/reduce_scatter | solution.py:265
  1113.9 870.0 %reduce-scatter.25.cloned.1.call-start = ((), (), s32[]{:S(2)}) async-start(), calls=%async_computation.15 | async-start | bytes 5898240 | tf_op jit(solution)/shard_map/reduce_scatter | solution.py:262
  1119.0 978.3 %reduce-scatter.23.cloned.1.call-start = ((), (), s32[]{:S(2)}) async-start(), calls=%async_computation.14 | async-start | bytes 5898240 | tf_op jit(solution)/shard_map/reduce_scatter | solution.py:262
  1124.0 1132.0 %all-reduce.20.cloned.1.call-start = ((), (), s32[]{:S(2)}) async-start(), calls=%async_computation.30 | async-start | bytes 10485760 | tf_op jit(solution)/shard_map/psum | solution.py:333
  2102.4 54.0 %copy-start.70 = (f32[128]{0:T(128)S(1)}, f32[128]{0:T(128)}, u32[]{:S(2)}) copy-start(f32[128]{0:T(128)} %copy-done.69) | copy-start | bytes 1540
  (75 other events, 685.4 us)
Sparse Core Ops, SparseCore 0:
  10.2 70.8 all-gather.28
  82.8 79.6 all-gather.30
  164.7 153.8 all-gather.32
  320.7 110.2 all-gather.34
  432.5 110.3 all-gather.36
  544.9 49.9 all-gather.38
  597.2 48.8 all-gather.40
  648.3 109.2 all-gather.44
  759.2 110.3 all-gather.46
  871.7 110.3 all-gather.42
  1083.3 126.4 all-reduce.21
  1212.7 49.5 reduce-scatter.20
  1264.8 49.2 reduce-scatter.18
  1317.0 49.2 reduce-scatter.16
  1369.3 49.2 reduce-scatter.14
  1420.9 109.8 reduce-scatter.30
  1533.0 110.9 reduce-scatter.32
  1646.2 110.9 reduce-scatter.28
  1759.6 110.9 reduce-scatter.26
  1872.9 110.9 reduce-scatter.24
  1986.3 110.9 reduce-scatter.22
  2101.4 154.4 all-reduce.19
where the time goes:
time: 2280 us; the launch traced here: 2270 us
  waiting for transfers between devices  1720 us (75%)
  blocking collectives  281 us (12%)
  matrix products  176 us (8%)
  local copies, waits for them, and re-layouts  38.4 us (2%)
  other arithmetic  33.2 us (1%)
    reduce_scatter x2, waiting for transfers between devices, shards(): lax.psum_scatter(grad_up_w.astype(jnp.bfloat16), 'group', scatter_dimensi...  224 us
    reduce_scatter x2, waiting for transfers between devices, shards(): lax.psum_scatter(grad_gate_w.astype(jnp.bfloat16), 'group', scatter_dimen...  224 us
    reduce_scatter x2, waiting for transfers between devices, shards(): lax.psum_scatter(grad_down_w.astype(jnp.bfloat16), 'group', scatter_dimen...  223 us
    all_gather x2, waiting for transfers between devices, fetch_mlp(): lax.all_gather(w_up[layer_index], 'group', axis=1, tiled=True)  215 us
    all_gather x2, waiting for transfers between devices, fetch_mlp(): lax.all_gather(w_down[layer_index], 'group', axis=0, tiled=True)  212 us
    all_gather x2, waiting for transfers between devices, fetch_mlp(): lax.all_gather(w_gate[layer_index], 'group', axis=1, tiled=True)  149 us
    all_gather x2, blocking collectives, fetch_attention(): lax.all_gather(w_value[layer_index], 'group', axis=0, tiled=True)  116 us
    reduce_scatter x2, waiting for transfers between devices, shards(): lax.psum_scatter(grad_query_w.astype(jnp.bfloat16), 'group', scatter_dime...  103 us
  transfers between devices with their start and end apart: 22, of which 20 were waited for; matrix products, arithmetic and copies ran while one was open for 6% of the time, Pallas kernels for 0%

commit v1 on v0

v1 whole, which is shorter than its diff:
```python
import functools

import jax
import jax.numpy as jnp
from jax import lax
from jax.experimental import pallas as pl
from jax.experimental.pallas import tpu as pltpu
from jax.sharding import PartitionSpec as P

Q_HEADS = 15
KV_HEADS = 5
HEAD = 64
LAYERS = 2
D = 960
SHARD = 120
PAD = 128
QKV = 1600
FFS = 320

norm_eps = 1e-05
rope_base = 100000.0
score_scale = 0.125
masked_value = -1e30
MESH = pl.DeviceIdType.MESH
BF = jnp.bfloat16
F32 = jnp.float32


def coords():
    r = lax.axis_index("replica")
    g = lax.axis_index("group")
    return r // 8, (r // 2) % 4, r % 2, g // 2, g % 2


def device(x_hi, z, core, y, x_lo):
    return ((x_hi * 4 + z) * 2 + core, y * 2 + x_lo)


def remote(src, dst, sems, index, target):
    return pltpu.make_async_remote_copy(
        src_ref=src,
        dst_ref=dst,
        send_sem=sems[0].at[index],
        recv_sem=sems[1].at[index],
        device_id=target,
        device_id_type=MESH,
    )


def greet(targets):
    barrier = pltpu.get_barrier_semaphore()
    for target in targets:
        pl.semaphore_signal(barrier, inc=1, device_id=target, device_id_type=MESH)
    pl.semaphore_wait(barrier, len(targets))


ANY = pl.BlockSpec(memory_space=pl.ANY)
VMEM = pl.BlockSpec(memory_space=pltpu.VMEM)


def gather_kernel(aq, ao, mg, md, fq, fo, fg, fd, send, recv, local):
    x_hi, z, core, y, x_lo = coords()
    sems = (send, recv)
    sibling = device(x_hi, z, 1 - core, y, x_lo)
    near = [device(x_hi, z, core, y, 1 - x_lo), device(1 - x_hi, z, core, y, 1 - x_lo)]
    ring = [None] + [device(x_hi, z, core, (y + k) % 4, x_lo) for k in (1, 2, 3)]
    greet(ring[1:] + near + [sibling])
    home = core == x_lo
    slot = [0]

    def index():
        slot[0] += 1
        return slot[0] - 1

    own_pairs = [(aq, fq), (ao, fo)]
    started = []

    first = []
    for l in range(LAYERS):
        for src, dst in own_pairs:
            first.append(remote(src.at[l], dst.at[l, y, core], sems, index(), near[l]))
    half_g, half_d = D // 2, FFS // 2
    rows_g = pl.ds(pl.multiple_of(core * half_g, 16), half_g)
    rows_d = pl.ds(pl.multiple_of(core * half_d, 16), half_d)
    other_g = pl.ds(pl.multiple_of((1 - core) * half_g, 16), half_g)
    other_d = pl.ds(pl.multiple_of((1 - core) * half_d, 16), half_d)
    swaps = []
    for l in range(LAYERS):
        swaps.append(
            [
                remote(mg.at[l, rows_g], fg.at[l, x_lo, rows_g], sems, index(), near[l]),
                remote(md.at[l, rows_d], fd.at[l, x_lo, rows_d], sems, index(), near[l]),
            ]
        )
    keeps = []
    for l in range(LAYERS):
        for k, (src, dst) in enumerate(own_pairs):
            keeps.append(pltpu.make_async_copy(src.at[l], dst.at[l, y, core], local.at[l * 4 + k]))
    keeps_m = []
    for l in range(LAYERS):
        for k, (src, dst) in enumerate([(mg, fg), (md, fd)]):
            keeps_m.append(pltpu.make_async_copy(src.at[l], dst.at[l, x_lo], local.at[l * 4 + 2 + k]))

    @pl.when(home)
    def _():
        for copy in first:
            copy.start()
        for copy in keeps:
            copy.start()

    for swap in swaps:
        for copy in swap:
            copy.start()
    for copy in keeps_m:
        copy.start()

    ring_copies = {}
    for l in range(LAYERS):

        @pl.when(home)
        def _():
            for copy in keeps[2 * l : 2 * l + 2]:
                copy.wait()

        @pl.when(jnp.logical_not(home))
        def _():
            for copy in first[2 * l : 2 * l + 2]:
                copy.wait_recv()

        for k in (1, 3, 2):
            for f in (fq, fo):
                copy = remote(f.at[l, y, core], f.at[l, y, core], sems, index(), ring[k])
                copy.start()
                ring_copies[l, k, f is fq] = copy
        for f in (fq, fo):
            copy = remote(f.at[l, y, core], f.at[l, y, core], sems, index(), sibling)
            copy.start()
            started.append(copy)
    for l in range(LAYERS):
        for k in (1, 3, 2):
            for f in (fq, fo):
                came = (y - k) % 4
                ring_copies[l, k, f is fq].wait_recv()
                copy = remote(f.at[l, came, core], f.at[l, came, core], sems, index(), sibling)
                copy.start()
                started.append(copy)
    for l in range(LAYERS):
        for copy, f, rows in zip(swaps[l], (fg, fd), (rows_g, rows_d)):
            copy.wait_recv()
            passed = remote(
                f.at[l, 1 - x_lo, rows], f.at[l, 1 - x_lo, rows], sems, index(), sibling
            )
            passed.start()
            started.append(passed)

    @pl.when(home)
    def _():
        for copy in first:
            copy.wait_send()

    for swap in swaps:
        for copy in swap:
            copy.wait_send()
    for copy in keeps_m:
        copy.wait()
    for copy in ring_copies.values():
        copy.wait_send()
    for copy in started:
        copy.wait()


def gather(aq, ao, mg, md):
    count = 40
    return pl.pallas_call(
        gather_kernel,
        out_shape=(
            jax.ShapeDtypeStruct((LAYERS, 4, 2, PAD, QKV), BF),
            jax.ShapeDtypeStruct((LAYERS, 4, 2, PAD, D), BF),
            jax.ShapeDtypeStruct((LAYERS, 2, D, 2 * FFS), BF),
            jax.ShapeDtypeStruct((LAYERS, 2, FFS, D), BF),
        ),
        in_specs=[ANY] * 4,
        out_specs=[ANY] * 4,
        scratch_shapes=[
            pltpu.SemaphoreType.DMA((count,)),
            pltpu.SemaphoreType.DMA((count,)),
            pltpu.SemaphoreType.DMA((8,)),
        ],
        compiler_params=pltpu.CompilerParams(collective_id=1, has_side_effects=True),
    )(aq, ao, mg, md)


def spread_kernel(x, out, send, recv):
    x_hi, z, core, y, x_lo = coords()
    targets = [device(x_hi, z, core, (y + k) % 4, x_lo) for k in (1, 3, 2)]
    greet(targets)
    copies = [
        remote(x, out.at[y], (send, recv), k, target) for k, target in enumerate(targets)
    ]
    for copy in copies:
        copy.start()
    out[y] = x[...]
    for copy in copies:
        copy.wait()


def spread(x):
    return pl.pallas_call(
        spread_kernel,
        out_shape=jax.ShapeDtypeStruct((4,) + x.shape, x.dtype),
        in_specs=[VMEM],
        out_specs=VMEM,
        scratch_shapes=[pltpu.SemaphoreType.DMA((3,)), pltpu.SemaphoreType.DMA((3,))],
        compiler_params=pltpu.CompilerParams(collective_id=2, has_side_effects=True),
    )(x)


def collect_kernel(x, base, out, came, send, recv):
    x_hi, z, core, y, x_lo = coords()
    targets = [device(x_hi, z, core, (y + k) % 4, x_lo) for k in (1, 3, 2)]
    greet(targets)
    copies = [
        remote(x.at[(y + k) % 4], came.at[i], (send, recv), i, targets[i])
        for i, k in enumerate((1, 3, 2))
    ]
    for copy in copies:
        copy.start()
    total = base[...] + x[y].astype(F32)
    for i, copy in enumerate(copies):
        copy.wait()
        total = total + came[i].astype(F32)
    out[...] = total


def collect(x, base):
    return pl.pallas_call(
        collect_kernel,
        out_shape=jax.ShapeDtypeStruct(base.shape, F32),
        in_specs=[VMEM, VMEM],
        out_specs=VMEM,
        scratch_shapes=[
            pltpu.VMEM((3,) + base.shape, BF),
            pltpu.SemaphoreType.DMA((3,)),
            pltpu.SemaphoreType.DMA((3,)),
        ],
        compiler_params=pltpu.CompilerParams(collective_id=3, has_side_effects=True),
    )(x, base)


def add_into(dst, others, step=16):
    rows = dst.shape[0]

    def body(i, carry):
        at = pl.ds(pl.multiple_of(i * step, step), step)
        total = dst[at, :].astype(F32)
        for other in others:
            total = total + other[at, :].astype(F32)
        dst[at, :] = total.astype(dst.dtype)
        return carry

    lax.fori_loop(0, rows // step, body, 0)


def add_to(dst, terms, step=16):
    rows = dst.shape[0]

    def body(i, carry):
        at = pl.ds(pl.multiple_of(i * step, step), step)
        total = terms[0][at, :].astype(F32)
        for other in terms[1:]:
            total = total + other[at, :].astype(F32)
        dst[at, :] = total.astype(dst.dtype)
        return carry

    lax.fori_loop(0, rows // step, body, 0)


def reduce_kernel(
    gq, go, gg, gd,
    fq, fo, fg, fd,
    sq, so, sg, sd,
    xq, xo, xg, xd,
    yq, yo,
    lq, lo,
    zq, zo, zg, zd,
    pq, po, pg, pd,
    hq, ho, hg, hd,
    send, recv,
):
    x_hi, z, core, y, x_lo = coords()
    sems = (send, recv)
    sibling = device(x_hi, z, 1 - core, y, x_lo)
    near = [device(x_hi, z, core, y, 1 - x_lo), device(1 - x_hi, z, core, y, 1 - x_lo)]
    far = device(1 - x_hi, z, core, y, x_lo)
    ring_y = {k: device(x_hi, z, core, (y + k) % 4, x_lo) for k in (1, 2, 3)}
    ring_z = {k: device(x_hi, (z + k) % 4, core, y, x_lo) for k in (1, 2, 3)}
    greet(list(ring_y.values()) + list(ring_z.values()) + near + [far, sibling])
    home = core == x_lo
    slot = [0]

    def index():
        slot[0] += 1
        return slot[0] - 1

    layers = (1, 0)
    pair = {}
    for l in layers:
        pair[l] = [
            remote(gg.at[l, 1 - core], sg.at[l], sems, index(), sibling),
            remote(gd.at[l, 1 - core], sd.at[l], sems, index(), sibling),
            remote(gq.at[l, :, 1 - core], sq.at[l], sems, index(), sibling),
            remote(go.at[l, :, 1 - core], so.at[l], sems, index(), sibling),
        ]
        for copy in pair[l]:
            copy.start()
    over_x = {}
    for l in layers:
        over_x[l] = [
            remote(src.at[l], dst.at[l], sems, index(), near[l])
            for src, dst in ((sg, xg), (sd, xd), (sq, xq), (so, xo))
        ]
    for l in layers:
        for k, (own, total) in enumerate(((gg, sg), (gd, sd), (gq, sq), (go, so))):
            pair[l][k].wait_recv()
            if k < 2:
                add_into(total.at[l], [own.at[l, core]])
            else:
                for q in range(4):
                    add_into(total.at[l, q], [own.at[l, q, core]])

            @pl.when(jnp.logical_not(home))
            def _():
                over_x[l][k].start()

    over_y = {}
    over_z = {}
    out_z = {}
    over_h = {}
    for l in layers:
        for k in (1, 3, 2):
            over_y[l, k] = [
                remote(sq.at[l, (y + k) % 4], yq.at[l, k - 1], sems, index(), ring_y[k]),
                remote(so.at[l, (y + k) % 4], yo.at[l, k - 1], sems, index(), ring_y[k]),
            ]

    def part(rows, where):
        return pl.ds(pl.multiple_of(where * (rows // 4), 16), rows // 4)

    pieces = ((sg, zg, pg, hg, fg, D), (sd, zd, pd, hd, fd, FFS), (lq, zq, pq, hq, fq, PAD), (lo, zo, po, ho, fo, PAD))
    for l in layers:
        for m, (src, zb, pb, hb, fb, rows) in enumerate(pieces):
            for k in (1, 3, 2):
                over_z[l, m, k] = remote(
                    src.at[l, part(rows, (z + k) % 4)], zb.at[l, k - 1], sems, index(), ring_z[k]
                )
            over_h[l, m] = remote(pb.at[l], hb.at[l], sems, index(), far)
            for k in (1, 3, 2):
                out_z[l, m, k] = remote(
                    fb.at[l, part(rows, z)], fb.at[l, part(rows, z)], sems, index(), ring_z[k]
                )
    last = {
        (l, m): remote(piece[4].at[l], piece[4].at[l], sems, index(), sibling)
        for l in layers
        for m, piece in enumerate(pieces)
    }

    @pl.when(home)
    def _():
        for l in layers:
            over_x[l][0].wait_recv()
            add_into(sg.at[l], [xg.at[l]])
            over_x[l][1].wait_recv()
            add_into(sd.at[l], [xd.at[l]])
            for m in (0, 1):
                for k in (1, 3, 2):
                    over_z[l, m, k].start()
            over_x[l][2].wait_recv()
            over_x[l][3].wait_recv()
            for k in (1, 3, 2, 0):
                for total, came in ((sq, xq), (so, xo)):
                    add_into(total.at[l, (y + k) % 4], [came.at[l, (y + k) % 4]])
                if k:
                    for copy in over_y[l, k]:
                        copy.start()
        for l in layers:
            for k in (1, 3, 2):
                for copy in over_y[l, k]:
                    copy.wait_recv()
            add_to(lq.at[l], [sq.at[l, y]] + [yq.at[l, j] for j in range(3)])
            add_to(lo.at[l], [so.at[l, y]] + [yo.at[l, j] for j in range(3)])
            for m in (2, 3):
                for k in (1, 3, 2):
                    over_z[l, m, k].start()
        for l in layers:
            for m, (src, zb, pb, hb, fb, rows) in enumerate(pieces):
                for k in (1, 3, 2):
                    over_z[l, m, k].wait_recv()
                add_to(pb.at[l], [src.at[l, part(rows, z)]] + [zb.at[l, j] for j in range(3)])
                over_h[l, m].start()
        for l in layers:
            for m, (src, zb, pb, hb, fb, rows) in enumerate(pieces):
                over_h[l, m].wait_recv()
                add_to(fb.at[l, part(rows, z)], [pb.at[l], hb.at[l]])
                for k in (1, 3, 2):
                    out_z[l, m, k].start()
        for l in layers:
            for m in range(4):
                for k in (1, 3, 2):
                    out_z[l, m, k].wait_recv()
                last[l, m].start()
        for l in layers:
            for m in range(4):
                last[l, m].wait_send()
                over_h[l, m].wait_send()
                for k in (1, 3, 2):
                    over_z[l, m, k].wait_send()
                    out_z[l, m, k].wait_send()
            for k in (1, 3, 2):
                for copy in over_y[l, k]:
                    copy.wait_send()

    @pl.when(jnp.logical_not(home))
    def _():
        for l in layers:
            for copy in over_x[l]:
                copy.wait_send()
        for copy in last.values():
            copy.wait_recv()

    for l in layers:
        for copy in pair[l]:
            copy.wait_send()


def reduce(gq, go, gg, gd):
    count = 144
    L = LAYERS

    def buf(*shape):
        return pltpu.VMEM(shape, BF)

    return pl.pallas_call(
        reduce_kernel,
        out_shape=(
            jax.ShapeDtypeStruct((L, PAD, QKV), BF),
            jax.ShapeDtypeStruct((L, PAD, D), BF),
            jax.ShapeDtypeStruct((L, D, 2 * FFS), BF),
            jax.ShapeDtypeStruct((L, FFS, D), BF),
        ),
        in_specs=[VMEM] * 4,
        out_specs=[VMEM] * 4,
        scratch_shapes=[
            buf(L, 4, PAD, QKV), buf(L, 4, PAD, D), buf(L, D, 2 * FFS), buf(L, FFS, D),
            buf(L, 4, PAD, QKV), buf(L, 4, PAD, D), buf(L, D, 2 * FFS), buf(L, FFS, D),
            buf(L, 3, PAD, QKV), buf(L, 3, PAD, D),
            buf(L, PAD, QKV), buf(L, PAD, D),
            buf(L, 3, PAD // 4, QKV), buf(L, 3, PAD // 4, D), buf(L, 3, D // 4, 2 * FFS), buf(L, 3, FFS // 4, D),
            buf(L, PAD // 4, QKV), buf(L, PAD // 4, D), buf(L, D // 4, 2 * FFS), buf(L, FFS // 4, D),
            buf(L, PAD // 4, QKV), buf(L, PAD // 4, D), buf(L, D // 4, 2 * FFS), buf(L, FFS // 4, D),
            pltpu.SemaphoreType.DMA((count,)),
            pltpu.SemaphoreType.DMA((count,)),
        ],
        compiler_params=pltpu.CompilerParams(
            collective_id=4, has_side_effects=True, vmem_limit_bytes=62 * 2**20
        ),
    )(gq, go, gg, gd)


def rms_scale(stream, gain_vec):
    return (
        stream * lax.rsqrt(jnp.mean(stream * stream, axis=-1, keepdims=True) + norm_eps) * gain_vec
    )


def rope_tables(positions):
    steps_half = jnp.arange(HEAD // 2, dtype=jnp.float32)
    inverse = rope_base ** (-2.0 * steps_half / HEAD)
    angles = positions[:, None] * inverse[None, :]
    cosine = jnp.cos(angles)
    sine_table = jnp.sin(angles)
    return (
        jnp.concatenate([cosine, cosine], axis=1),
        jnp.concatenate([sine_table, sine_table], axis=1),
    )


def rotate(values, cosine, sine_table):
    amount = values.shape[0]
    shaped = values.reshape(amount, -1, HEAD)
    first_half = shaped[..., : HEAD // 2]
    second_half = shaped[..., HEAD // 2 :]
    turned = jnp.concatenate([-second_half, first_half], axis=-1)
    return (shaped * cosine[:, None, :] + turned * sine_table[:, None, :]).reshape(values.shape)


def rotate_back(grad_values, cosine, sine_table):
    amount = grad_values.shape[0]
    shaped = grad_values.reshape(amount, -1, HEAD)
    scaled = shaped * sine_table[:, None, :]
    turned = jnp.concatenate([scaled[..., HEAD // 2 :], -scaled[..., : HEAD // 2]], axis=-1)
    return (shaped * cosine[:, None, :] + turned).reshape(grad_values.shape)


def layout(seq_lengths, amount):
    finish = jnp.cumsum(seq_lengths)
    indices = jnp.arange(amount, dtype=jnp.int32)
    documents = jnp.sum((indices[:, None] >= finish[None, :]).astype(jnp.int32), axis=1)
    starts = finish - seq_lengths
    member = documents[:, None] == jnp.arange(seq_lengths.shape[0], dtype=jnp.int32)[None, :]
    begins = jnp.sum(jnp.where(member, starts[None, :], 0), axis=1)
    return (documents, indices - begins)


def times_transposed(left_side, right_side):
    return lax.dot_general(
        left_side, right_side, (((1,), (1,)), ((), ())), preferred_element_type=jnp.float32
    )


def transposed_times(left_side, right_side):
    return lax.dot_general(
        left_side, right_side, (((0,), (0,)), ((), ())), preferred_element_type=jnp.float32
    )


def split_queries(query_rows):
    own_rows = query_rows.shape[0]
    share = Q_HEADS // KV_HEADS
    return (
        query_rows.reshape(own_rows, KV_HEADS, share, HEAD)
        .transpose(1, 2, 0, 3)
        .reshape(KV_HEADS, share * own_rows, HEAD)
    )


def join_queries(rows):
    share = Q_HEADS // KV_HEADS
    own_rows = rows.shape[1] // share
    return (
        rows.reshape(KV_HEADS, share, own_rows, HEAD)
        .transpose(2, 0, 1, 3)
        .reshape(own_rows, Q_HEADS * HEAD)
    )


def split_keys(key_rows):
    return key_rows.reshape(key_rows.shape[0], KV_HEADS, HEAD).transpose(1, 0, 2)


def join_keys(rows):
    return rows.transpose(1, 0, 2).reshape(rows.shape[1], KV_HEADS * HEAD)


def bdot(a, b, ca, cb):
    return lax.dot_general(a, b, (((ca,), (cb,)), ((0,), (0,))), preferred_element_type=F32)


def attention_weights(query_heads, key_heads, allowed):
    scores = bdot(query_heads, key_heads, 2, 2) * score_scale
    scores = jnp.where(allowed[None], scores, masked_value)
    weights = jnp.exp(scores - jnp.max(scores, axis=-1, keepdims=True))
    return weights / jnp.sum(weights, axis=-1, keepdims=True)


def attention_forward(query_rot, key_rot, values, allowed):
    soft = attention_weights(split_queries(query_rot), split_keys(key_rot), allowed)
    mixed = bdot(soft.astype(BF), split_keys(values), 2, 1)
    return join_queries(mixed.astype(BF))


def attention_backward(query_rot, key_rot, values, grad_mixed, allowed):
    q, k, v = split_queries(query_rot), split_keys(key_rot), split_keys(values)
    g = split_queries(grad_mixed)
    soft = attention_weights(q, k, allowed)
    grad_probs = bdot(g, v, 2, 2)
    inner = jnp.sum(soft * grad_probs, axis=-1, keepdims=True)
    grad_scores = (soft * (grad_probs - inner)).astype(BF)
    grad_query = bdot(grad_scores, k, 2, 1) * score_scale
    grad_key = bdot(grad_scores, q, 1, 1) * score_scale
    grad_value = bdot(soft.astype(BF), g, 1, 1)
    return join_queries(grad_query), join_keys(grad_key), join_keys(grad_value)


def pad_cols(a):
    rows = a.shape[0]
    a = a.reshape(rows, 8, SHARD)
    return jnp.pad(a, ((0, 0), (0, 0), (0, PAD - SHARD))).reshape(rows, 8 * PAD)


def unpad_cols(a):
    rows = a.shape[0]
    return a.reshape(rows, 8, PAD)[:, :, :SHARD].reshape(rows, D)


def dot(a, b):
    return jnp.dot(a, b, preferred_element_type=F32)


def shards(
    tokens, cotangent, lengths, gain_attn, w_query, w_key, w_value, w_out, gain_mlp, w_gate, w_up, w_down
):
    own_rows = tokens.shape[0]
    doc_own, pos_own = layout(lengths[0], own_rows)
    cosine, sine_table = rope_tables(pos_own.astype(F32))
    row_index = jnp.arange(own_rows, dtype=jnp.int32)
    allowed = (doc_own[:, None] == doc_own[None, :]) & (row_index[None, :] <= row_index[:, None])
    allowed3 = jnp.concatenate([allowed] * (Q_HEADS // KV_HEADS), axis=0)

    gains = jnp.stack([gain_attn, gain_mlp], axis=1)
    gains = jnp.pad(gains, ((0, 0), (0, PAD - SHARD - 2), (0, QKV - SHARD)))
    packed_qkv = jnp.concatenate(
        [jnp.concatenate([w_query, w_key, w_value], axis=2), gains], axis=1
    )
    packed_out = jnp.pad(w_out, ((0, 0), (0, PAD - SHARD), (0, 0)))
    packed_gu = jnp.concatenate([w_gate, w_up], axis=2)
    fq, fo, fg, fd = gather(packed_qkv, packed_out, packed_gu, w_down)
    all_gains = fq[:, :, :, SHARD : SHARD + 2, :SHARD].reshape(LAYERS, 8, 2, SHARD)
    gain_one = all_gains[:, :, 0].reshape(LAYERS, D).astype(F32)
    gain_two = all_gains[:, :, 1].reshape(LAYERS, D).astype(F32)
    full_qkv = fq.reshape(LAYERS, 8 * PAD, QKV)
    full_out = fo.reshape(LAYERS, 8 * PAD, D)

    stream = tokens.astype(F32)
    saved = []
    for l in range(LAYERS):
        normed = rms_scale(stream, gain_one[l]).astype(BF)
        normed_pad = pad_cols(normed)
        proj = dot(normed_pad, full_qkv[l])
        query_rot = rotate(proj[:, :D], cosine, sine_table).astype(BF)
        key_rot = rotate(proj[:, D : D + FFS], cosine, sine_table).astype(BF)
        values = proj[:, D + FFS :].astype(BF)
        mixed_low = attention_forward(query_rot, key_rot, values, allowed3)
        mixed_pad = pad_cols(mixed_low)
        hidden = stream + dot(mixed_pad, full_out[l])
        normed_two = rms_scale(hidden, gain_two[l]).astype(BF)
        mlp_in = spread(normed_two).reshape(4 * own_rows, D)
        pre = [dot(mlp_in, fg[l, p]) for p in range(2)]
        active = []
        for p in range(2):
            gate, up = pre[p][:, :FFS], pre[p][:, FFS:]
            active.append((gate * jax.nn.sigmoid(gate) * up).astype(BF))
        partial = sum(dot(active[p], fd[l, p]) for p in range(2))
        result = collect(partial.astype(BF).reshape(4, own_rows, D), hidden)
        saved.append((stream, hidden, normed_pad, query_rot, key_rot, values, mixed_pad, mlp_in, pre, active))
        stream = result

    grad_stream = cotangent.astype(F32)
    zero = jnp.zeros((own_rows, D), F32)
    collected = [None] * LAYERS
    for l in reversed(range(LAYERS)):
        layer_in, hidden, normed_pad, query_rot, key_rot, values, mixed_pad, mlp_in, pre, active = saved[l]
        grad_low = spread(grad_stream.astype(BF)).reshape(4 * own_rows, D)
        grad_in = 0.0
        grads_gu, grads_d = [], []
        for p in range(2):
            gate, up = pre[p][:, :FFS], pre[p][:, FFS:]
            sig = jax.nn.sigmoid(gate)
            grad_active = times_transposed(grad_low, fd[l, p])
            grad_gate = grad_active * up * sig * (1.0 + gate * (1.0 - sig))
            grad_up = grad_active * gate * sig
            both = jnp.concatenate([grad_gate, grad_up], axis=1).astype(BF)
            grad_in = grad_in + times_transposed(both, fg[l, p])
            grads_gu.append(transposed_times(mlp_in, both).astype(BF))
            grads_d.append(transposed_times(active[p], grad_low).astype(BF))
        grad_input = collect(grad_in.astype(BF).reshape(4, own_rows, D), zero)
        norm_value, norm_back = jax.vjp(rms_scale, hidden, gain_two[l])
        grad_hidden_norm, grad_gain_two = norm_back(grad_input)
        grad_hidden = grad_stream + grad_hidden_norm
        grad_hidden_low = grad_hidden.astype(BF)
        grad_mixed = unpad_cols(times_transposed(grad_hidden_low, full_out[l]).astype(BF))
        grad_out = transposed_times(mixed_pad, grad_hidden_low).astype(BF)
        grad_query_rot, grad_key_rot, grad_values = attention_backward(
            query_rot, key_rot, values, grad_mixed, allowed3
        )
        grad_proj = jnp.concatenate(
            [
                rotate_back(grad_query_rot, cosine, sine_table),
                rotate_back(grad_key_rot, cosine, sine_table),
                grad_values,
            ],
            axis=1,
        ).astype(BF)
        grad_normed = unpad_cols(times_transposed(grad_proj, full_qkv[l]))
        norm_first, back_first = jax.vjp(rms_scale, layer_in, gain_one[l])
        grad_stream_norm, grad_gain_one = back_first(grad_normed)
        grad_stream = grad_hidden + grad_stream_norm
        grad_qkv = transposed_times(normed_pad, grad_proj).astype(BF).reshape(8, PAD, QKV)
        both_gains = jnp.stack([grad_gain_one.reshape(8, SHARD), grad_gain_two.reshape(8, SHARD)], axis=1)
        both_gains = jnp.pad(both_gains, ((0, 0), (0, PAD - SHARD - 2), (0, QKV - SHARD))).astype(BF)
        grad_qkv = jnp.concatenate([grad_qkv[:, :SHARD], both_gains], axis=1)
        collected[l] = (
            grad_qkv.reshape(4, 2, PAD, QKV),
            grad_out.reshape(4, 2, PAD, D),
            jnp.stack(grads_gu),
            jnp.stack(grads_d),
        )
    rq, ro, rg, rd = reduce(*[jnp.stack([collected[0][k], collected[1][k]]) for k in range(4)])
    rq, ro, rg, rd = (a.astype(F32) for a in (rq, ro, rg, rd))
    return (
        stream.astype(BF),
        grad_stream,
        rq[:, SHARD, :SHARD],
        rq[:, :SHARD, :D],
        rq[:, :SHARD, D : D + FFS],
        rq[:, :SHARD, D + FFS :],
        ro[:, :SHARD],
        rq[:, SHARD + 1, :SHARD],
        rg[:, :, :FFS],
        rg[:, :, FFS:],
        rd,
    )


def solution(mesh):
    in_specs = (
        P(("replica", "group"), None),
        P(("replica", "group"), None),
        P(("replica", "group"), None),
        P(None, "group"),
        P(None, "group", None),
        P(None, "group", None),
        P(None, "group", None),
        P(None, "group", None),
        P(None, "group"),
        P(None, None, "group"),
        P(None, None, "group"),
        P(None, "group", None),
    )
    out_specs = (
        P(("replica", "group"), None),
        P(("replica", "group"), None),
        P(None, "group"),
        P(None, "group", None),
        P(None, "group", None),
        P(None, "group", None),
        P(None, "group", None),
        P(None, "group"),
        P(None, None, "group"),
        P(None, None, "group"),
        P(None, "group", None),
    )
    return jax.shard_map(shards, mesh=mesh, in_specs=in_specs, out_specs=out_specs, check_vma=False)
```

time: 2280 us -> 653 us (0.29)
  waiting for transfers between devices: 1720 us -> 0 us
  Pallas kernels: 0 us -> 422 us
  blocking collectives: 281 us -> 0 us
  matrix products: 176 us -> 80.8 us
  local copies, waits for them, and re-layouts: 38.4 us -> 89.6 us
    reduce_scatter x10 -> x0, waiting for transfers between devices: 875 us -> none  [the longest x2 224 us: shards(): lax.psum_scatter(grad_up_w.astype(jnp.bfloat16), 'group', scatter_dimensi...]
    all_gather x10 -> x0, waiting for transfers between devices: 668 us -> none  [the longest x2 215 us: fetch_mlp(): lax.all_gather(w_up[layer_index], 'group', axis=1, tiled=True)]
    pallas_call x0 -> x10, Pallas kernels: none -> 422 us  [the longest x1 191 us: reduce(): pl.pallas_call(reduce_kernel, out_shape=(jax.ShapeDtypeStruct((L, PAD, QK...]
    all_gather x4 -> x0, blocking collectives: 211 us -> none  [the longest x2 116 us: fetch_attention(): lax.all_gather(w_value[layer_index], 'group', axis=0, tiled=True)]
    psum x1 -> x0, waiting for transfers between devices: 93.6 us -> none  [shards(): lax.psum(stacked[1].astype(jnp.bfloat16), 'replica').astype(jnp.float32)]
    unnamed x23 -> x0, waiting for transfers between devices: 88.4 us -> none
    dot_general x84 -> x22, matrix products: 108 us -> 35.4 us  [the longest x12 22.6 us: dot(): return jnp.dot(a, b, preferred_element_type=F32)]
    psum x1 -> x0, blocking collectives: 37 us -> none  [shards(): lax.psum(stacked[0].astype(jnp.bfloat16), 'replica').astype(jnp.float32)]
  transfers between devices with their start and end apart: 22 -> 0, of which waited for: 20 -> 0; matrix products, arithmetic and copies ran while one was open for 6% -> 0% of each run, Pallas kernels for 0% -> 0%
where the time goes in v1:
time: 653 us; the launch traced here: 642 us
  Pallas kernels  422 us (65%)
  local copies, waits for them, and re-layouts  89.6 us (14%)
  matrix products  80.8 us (12%)
  other arithmetic  47.1 us (7%)
    pallas_call x1, Pallas kernels, reduce(): pl.pallas_call(reduce_kernel, out_shape=(jax.ShapeDtypeStruct((L, PAD, QK...  191 us
    pallas_call x1, Pallas kernels, gather(): pl.pallas_call(gather_kernel, out_shape=(jax.ShapeDtypeStruct((LAYERS, 4,...  120 us
    pallas_call x4, Pallas kernels, collect(): pl.pallas_call(collect_kernel, out_shape=jax.ShapeDtypeStruct(base.shape,...  61.9 us
    pallas_call x4, Pallas kernels, spread(): pl.pallas_call(spread_kernel, out_shape=jax.ShapeDtypeStruct((4,) + x.sha...  48.3 us
    unnamed x216, local copies, waits for them, and re-layouts  30.2 us
    dot_general x12, matrix products, times_transposed(): lax.dot_general(left_side, right_side, (((1,), (1,)), ((), ())), preferre...  25.3 us
    dot_general x12, matrix products, dot(): return jnp.dot(a, b, preferred_element_type=F32)  22.6 us
    dot_general x12, matrix products, transposed_times(): lax.dot_general(left_side, right_side, (((0,), (0,)), ((), ())), preferre...  16.2 us

profile of v1, /device:TPU:1, one launch (start us, length us, event | category | flops | bytes accessed | tf_op | source)
XLA Modules:
  0.0 641.9 jit_solution(15936428473449965590)
XLA Ops:
  11.3 119.9 %shard_map.203 = (bf16[2,4,2,128,1600]{4,3,2,1,0:T(8,128)(2,1)}, bf16[2,4,2,128,960]{4,3,2,1,0:T(8,128)(2,1)}, bf16[2,2,960,640]{3,2,1,0:T(8,128)(2,1)}, bf16[2,2,320,960]{3,2,1,0:T(8,128)(2,1)}) custom-call(bf16[2,128,1600]{2,1,0:T(8,128)(2,1)} %pad_maximum_fusion.5.aq, bf16[2,128,960]{2,1,0:T(8,128)(2,1)} %pad.31.ao, ...), custom_call_target="tpu_custom_call" | custom-call | tf_op jit(solution)/shard_map/pallas_call | solution.py:174
  132.7 5.4 fusion.142
  144.1 4.3 fusion.143
  150.4 12.1 %shard_map.204 = bf16[4,128,960]{2,1,0:T(8,128)(2,1)} custom-call(bf16[128,960]{1,0:T(8,128)(2,1)} %multiply_convert_fusion.16.x), custom_call_target="tpu_custom_call" | custom-call | tf_op jit(solution)/shard_map/pallas_call | solution.py:208
  162.5 2.7 fusion.32
  165.5 2.6 fusion.36
  172.6 11.8 %shard_map.205 = f32[128,960]{1,0:T(8,128)} custom-call(bf16[4,128,960]{2,1,0:T(8,128)(2,1)} %bitcast.344, f32[128,960]{1,0:T(8,128)} %copy-done.6), custom_call_target="tpu_custom_call" | custom-call | tf_op jit(solution)/shard_map/pallas_call | solution.py:236
  187.5 3.5 fusion.154
  204.4 11.5 %shard_map.206 = bf16[4,128,960]{2,1,0:T(8,128)(2,1)} custom-call(bf16[128,960]{1,0:T(8,128)(2,1)} %multiply_convert_fusion.14.x), custom_call_target="tpu_custom_call" | custom-call | tf_op jit(solution)/shard_map/pallas_call | solution.py:208
  215.9 3.6 fusion.29
  221.4 13.1 %shard_map.208 = bf16[4,128,960]{2,1,0:T(8,128)(2,1)} custom-call(bf16[128,960]{1,0:T(8,128)(2,1)} %copy.270.x), custom_call_target="tpu_custom_call" | custom-call | tf_op jit(solution)/shard_map/pallas_call | solution.py:208
  234.5 3.6 multiply_convert_fusion.9
  242.5 2.6 multiply_convert_fusion.7
  251.2 17.0 %shard_map.209 = f32[128,960]{1,0:T(8,128)} custom-call(bf16[4,128,960]{2,1,0:T(8,128)(2,1)} %bitcast.341, f32[128,960]{1,0:T(8,128)} %broadcast_in_dim.53.base), custom_call_target="tpu_custom_call" | custom-call | tf_op jit(solution)/shard_map/pallas_call | solution.py:236
  281.4 2.4 convolution_convert_fusion.17
  283.9 4.0 fusion.8
  294.4 11.6 %shard_map.210 = bf16[4,128,960]{2,1,0:T(8,128)(2,1)} custom-call(bf16[128,960]{1,0:T(8,128)(2,1)} %get-tuple-element.94.x), custom_call_target="tpu_custom_call" | custom-call | tf_op jit(solution)/shard_map/pallas_call | solution.py:208
  324.6 2.7 pad_maximum_fusion.1.gg
  329.2 3.9 copy.305
  333.1 2.6 fusion.34
  335.7 3.2 add_convert_fusion
  341.2 15.9 %shard_map.211 = f32[128,960]{1,0:T(8,128)} custom-call(bf16[4,128,960]{2,1,0:T(8,128)(2,1)} %bitcast.342, f32[128,960]{1,0:T(8,128)} %broadcast_in_dim.53.base), custom_call_target="tpu_custom_call" | custom-call | tf_op jit(solution)/shard_map/pallas_call | solution.py:236
  362.5 3.9 copy.304
  366.3 4.7 pad_maximum_fusion.2.go
  380.6 3.8 copy.330
  395.8 3.6 copy.331
  403.7 3.5 pad_maximum_fusion.gq
  407.2 191.5 %shard_map.212 = (bf16[2,128,1600]{2,1,0:T(8,128)(2,1)}, bf16[2,128,960]{2,1,0:T(8,128)(2,1)}, bf16[2,960,640]{2,1,0:T(8,128)(2,1)}, bf16[2,320,960]{2,1,0:T(8,128)(2,1)}) custom-call(bf16[2,4,2,128,1600]{4,3,2,1,0:T(8,128)(2,1)} %pad_maximum_fusion.gq, bf16[2,4,2,128,960]{4,3,2,1,0:T(8,128)(2,1)} %pad_maximum_fusion.2.go, ...), custom_call_target="tpu_custom_call" | custom-call | tf_op jit(solution)/shard_map/pallas_call | solution.py:442
  598.7 4.1 fusion.144
  602.8 3.3 copy.310
  608.3 3.2 convert_element_type.227
  622.3 17.2 %shard_map.207 = f32[128,960]{1,0:T(8,128)} custom-call(bf16[4,128,960]{2,1,0:T(8,128)(2,1)} %bitcast.343, f32[128,960]{1,0:T(8,128)} %copy-done.5), custom_call_target="tpu_custom_call" | custom-call | tf_op jit(solution)/shard_map/pallas_call | solution.py:236
  (385 shorter events, 140.3 us)
Async XLA Ops:
  4.4 4.6 copy-start.50
  4.4 5.0 copy-start.90
  4.4 5.0 copy-start.91
  6.8 3.7 copy-start.49
  11.3 120.8 %copy-start.66 = (bf16[128,960]{0,1:T(8,128)(2,1)S(1)}, bf16[128,960]{0,1:T(8,128)(2,1)}, u32[]{:S(2)}) copy-start(bf16[128,960]{0,1:T(8,128)(2,1)} %param.12) | copy-start | bytes 737284
  132.3 5.8 copy-start.85
  132.4 5.8 copy-start.81
  132.7 5.4 copy-start.20
  144.1 4.3 copy-start.27
  149.0 16.2 %copy-start.6 = (f32[128,960]{1,0:T(8,128)}, f32[128,960]{1,0:T(8,128)S(1)}, u32[]{:S(2)}) copy-start(f32[128,960]{1,0:T(8,128)S(1)} %get-tuple-element.143.base) | copy-start | bytes 1474564
  149.0 16.2 %copy-start.83 = (f32[128]{0:T(128)}, f32[128]{0:T(128)S(1)}, u32[]{:S(2)}) copy-start(f32[128]{0:T(128)S(1)} %fusion.119) | copy-start | bytes 1540
  165.5 4.6 copy-start.18
  165.5 3.8 copy-start.23
  187.5 3.6 copy-start.21
  196.5 78.5 %copy-start.74 = (f32[5,384]{1,0:T(8,128)}, f32[5,384]{1,0:T(8,128)S(1)}, u32[]{:S(2)}) copy-start(f32[5,384]{1,0:T(8,128)S(1)} %get-tuple-element.144) | copy-start | bytes 23044
  197.2 4.1 copy-start.1
  203.5 66.7 %copy-start.5 = (f32[128,960]{1,0:T(8,128)}, f32[128,960]{1,0:T(8,128)S(1)}, u32[]{:S(2)}) copy-start(f32[128,960]{1,0:T(8,128)S(1)} %get-tuple-element.147.base) | copy-start | bytes 1474564
  234.5 6.8 %slice-start = ((s8[4915200]{0:T(1024)(128)(4,1)}), s8[4194304]{0:T(1024)(128)(4,1)S(1)}, s32[]{:S(2)}) async-start(s8[4915200]{0:T(1024)(128)(4,1)} %bitcast.361), calls=%async_computation | async-start | bytes 8388608
  234.5 6.8 %slice-start.1 = ((s8[4915200]{0:T(1024)(128)(4,1)}), s8[720896]{0:T(1024)(128)(4,1)S(1)}, s32[]{:S(2)}) async-start(s8[4915200]{0:T(1024)(128)(4,1)} %bitcast.361), calls=%async_computation.1 | async-start | bytes 1441792
  268.3 4.0 copy-start
  283.9 6.0 copy-start.80
  283.9 8.4 %copy-start.14 = (f32[128,960]{1,0:T(8,128)S(1)}, f32[128,960]{1,0:T(8,128)}, u32[]{:S(2)}) copy-start(f32[128,960]{1,0:T(8,128)} %copy-done.13) | copy-start | bytes 1474564
  294.4 13.4 %copy-start.17 = (bf16[512,320]{1,0:T(8,128)(2,1)S(1)}, bf16[512,320]{1,0:T(8,128)(2,1)}, u32[]{:S(2)}) copy-start(bf16[512,320]{1,0:T(8,128)(2,1)} %copy-done.16) | copy-start | bytes 983044
  338.9 18.3 %copy-start.7 = (f32[128,960]{1,0:T(8,128)S(1)}, f32[128,960]{1,0:T(8,128)}, u32[]{:S(2)}) copy-start(f32[128,960]{1,0:T(8,128)} %copy-done.6) | copy-start | bytes 1474564
  338.9 18.3 %copy-start.84 = (f32[128]{0:T(128)S(1)}, f32[128]{0:T(128)}, u32[]{:S(2)}) copy-start(f32[128]{0:T(128)} %copy-done.83) | copy-start | bytes 1540
  338.9 20.1 %copy-start.89 = (f32[128]{0:T(128)S(1)}, f32[128]{0:T(128)}, u32[]{:S(2)}) copy-start(f32[128]{0:T(128)} %copy-done.88) | copy-start | bytes 1540
  360.4 10.6 %copy-start.11 = (f32[128,960]{1,0:T(8,128)}, f32[128,960]{1,0:T(8,128)S(1)}, u32[]{:S(2)}) copy-start(f32[128,960]{1,0:T(8,128)S(1)} %fusion.72) | copy-start | bytes 1474564
  387.4 3.9 copy-start.82
  387.4 5.2 copy-start.78
  611.7 4.5 copy-start.86
  611.7 4.5 copy-start.12
  611.7 4.5 copy-start.15
  (69 other events, 126.7 us)

commit v2 on v0

v2 whole, which is shorter than its diff:
```python
import functools

import jax
import jax.numpy as jnp
from jax import lax
from jax.experimental import pallas as pl
from jax.experimental.pallas import tpu as pltpu
from jax.sharding import PartitionSpec as P

Q_HEADS = 15
KV_HEADS = 5
HEAD = 64
LAYERS = 2
D = 960
SHARD = 120
PAD = 128
QKV = 1600
FFS = 320

norm_eps = 1e-05
rope_base = 100000.0
score_scale = 0.125
masked_value = -1e30
MESH = pl.DeviceIdType.MESH
BF = jnp.bfloat16
F32 = jnp.float32


def coords():
    r = lax.axis_index("replica")
    g = lax.axis_index("group")
    return r // 8, (r // 2) % 4, r % 2, g // 2, g % 2


def device(x_hi, z, core, y, x_lo):
    return ((x_hi * 4 + z) * 2 + core, y * 2 + x_lo)


def remote(src, dst, sems, index, target):
    return pltpu.make_async_remote_copy(
        src_ref=src,
        dst_ref=dst,
        send_sem=sems[0].at[index],
        recv_sem=sems[1].at[index],
        device_id=target,
        device_id_type=MESH,
    )


def greet(targets):
    barrier = pltpu.get_barrier_semaphore()
    for target in targets:
        pl.semaphore_signal(barrier, inc=1, device_id=target, device_id_type=MESH)
    pl.semaphore_wait(barrier, len(targets))


ANY = pl.BlockSpec(memory_space=pl.ANY)
VMEM = pl.BlockSpec(memory_space=pltpu.VMEM)
ROWS = 128
KV = KV_HEADS * HEAD
SHARE = Q_HEADS // KV_HEADS


def dot(a, b):
    return lax.dot_general(a, b, (((1,), (0,)), ((), ())), preferred_element_type=F32)


def dot_t(a, b):
    return lax.dot_general(a, b, (((1,), (1,)), ((), ())), preferred_element_type=F32)


def t_dot(a, b):
    return lax.dot_general(a, b, (((0,), (0,)), ((), ())), preferred_element_type=F32)


def lanes(g, width):
    return pl.ds(pl.multiple_of(g * PAD, PAD), width)


def halves(a):
    high = a.astype(BF)
    return high, (a - high.astype(F32)).astype(BF)


class Slots:
    def __init__(self):
        self.used = 0

    def take(self, count=1):
        self.used += count
        return self.used - count


def order(k):
    return k + (k // 2) * (5 - 2 * k)


def step_kernel(
    tokens, cotangent, cosine, sine, bias, gains,
    wq, wk, wv, wo, wg, wu, wd,
    out_act, out_grad, gq, gk, gv, go, gg, gu, gd,
    fq, fk, fv, fo, fg, fu, fd, fgain,
    place, gain_full, gain_pad, stream, hidden, grad, wide, narrow, wide_pad,
    npad, mpad, qrot, krot, vals, mixed, gproj_q, gproj_k, gproj_v, gmix,
    acts_in, grads_in, parts, came,
    s_gate, s_up, s_act, s_gg, s_gu, tg, tu, td, own_part, glow, gain_grad,
    send, recv, local,
):
    x_hi, z, core, y, x_lo = coords()
    sems = (send, recv)
    slots = Slots()
    sibling = device(x_hi, z, 1 - core, y, x_lo)
    near = [device(x_hi, z, core, y, 1 - x_lo), device(1 - x_hi, z, core, y, 1 - x_lo)]

    def along_y(k):
        return device(x_hi, z, core, (y + k) % 4, x_lo)

    greet(
        [device(x_hi, z, core, (y + k) % 4, (x_lo + e) % 2) for k in range(4) for e in range(2) if k + e]
        + [near[1], sibling]
    )
    home = core == x_lo
    guest = jnp.logical_not(home)

    slabs = [(wq, fq, 0), (wk, fk, 1), (wv, fv, 1), (wo, fo, 1)]
    keep, ring, cross, swap_cores = {}, {}, {}, {}
    for l in range(LAYERS):
        for a, (src, dst, side) in enumerate(slabs):
            keep[l, a] = pltpu.make_async_copy(src.at[l], dst.at[l, y, core], local.at[l * 8 + a])
            for k in (1, 2, 3):
                ring[l, a, k] = remote(src.at[l], dst.at[l, y, core], sems, slots.take(), along_y(k))
            for k in range(4):
                at = dst.at[l, (y - k) % 4, core]
                cross[l, a, k] = remote(
                    src.at[l] if k == 0 else at, at, sems, slots.take(), near[side]
                )
                swap_cores[l, a, k] = remote(at, at, sems, slots.take(), sibling)
    own_gain = fgain.at[y, x_lo]
    gain_keep = pltpu.make_async_copy(gains, own_gain, local.at[16])
    members = [(k, e) for k in range(4) for e in range(2) if k + e > 0]

    def member(k, e):
        return device(x_hi, z, core, (y + k) % 4, (x_lo + e) % 2)

    gain_send = {
        (k, e): remote(gains, own_gain, sems, slots.take(), member(k, e)) for k, e in members
    }
    half_g, half_d = D // 2, FFS // 2
    rows_g = pl.ds(pl.multiple_of(core * half_g, 16), half_g)
    rows_d = pl.ds(pl.multiple_of(core * half_d, 16), half_d)
    pairs = [(wg, fg, rows_g), (wu, fu, rows_g), (wd, fd, rows_d)]
    keep_m, cross_m, pass_m = {}, {}, {}
    for l in range(LAYERS):
        for a, (src, dst, rows) in enumerate(pairs):
            keep_m[l, a] = pltpu.make_async_copy(src.at[l], dst.at[l, x_lo], local.at[l * 8 + 4 + a])
            cross_m[l, a] = remote(src.at[l, rows], dst.at[l, x_lo, rows], sems, slots.take(), near[l])
            there = dst.at[l, 1 - x_lo, rows]
            pass_m[l, a] = remote(there, there, sems, slots.take(), sibling)

    def gather_begin(l, arrays):
        @pl.when(home)
        def _():
            for a in arrays:
                for k in (1, 3, 2):
                    ring[l, a, k].start()
                cross[l, a, 0].start()
                keep[l, a].start()

    def gather_pass(l, arrays):
        for a in arrays:

            @pl.when(home)
            def _():
                keep[l, a].wait()
                swap_cores[l, a, 0].start()
                for k in (1, 3, 2):
                    ring[l, a, k].wait_recv()
                    cross[l, a, k].start()
                    swap_cores[l, a, k].start()

            @pl.when(guest)
            def _():
                for k in (0, 1, 3, 2):
                    cross[l, a, k].wait_recv()
                    swap_cores[l, a, k].start()

    def gather_end(l, arrays):
        for a in arrays:
            for k in range(4):
                swap_cores[l, a, k].wait_recv()

    def gather_sent(l, arrays):
        for a in arrays:

            @pl.when(home)
            def _():
                for k in (1, 2, 3):
                    ring[l, a, k].wait_send()
                for k in range(4):
                    cross[l, a, k].wait_send()

            for k in range(4):
                swap_cores[l, a, k].wait_send()

    def pairs_begin(l):
        for a in range(3):
            cross_m[l, a].start()
            keep_m[l, a].start()

    def pairs_pass(l):
        for a in range(3):
            cross_m[l, a].wait_recv()
            pass_m[l, a].start()

    def pairs_end(l):
        for a in range(3):
            pass_m[l, a].wait_recv()
            keep_m[l, a].wait()

    spread_at = [slots.take(4) for _ in range(4)]
    back_at = [slots.take(4) for _ in range(4)]

    def spread_copy(n, buffer, k):
        return remote(
            buffer.at[y], buffer.at[y], sems, spread_at[n] + k, along_y(k)
        )

    def spread(n, buffer):
        for k in (1, 3, 2):
            spread_copy(n, buffer, k).start()

    def arrived(n, buffer, k):
        there = buffer.at[(y - k + 4) % 4]
        remote(there, there, sems, spread_at[n] + k, along_y(k)).wait_recv()

    def back_copy(n, k):
        return remote(
            parts.at[n % 2, k - 1], came.at[n % 2, k - 1], sems, back_at[n] + k, along_y(4 - k)
        )

    def collect(n, total):
        for k in (1, 3, 2):
            back_copy(n, k).wait_recv()
            total = total + came[n % 2, k - 1].astype(F32)
        return total

    def sent(n, buffer):
        for k in (1, 2, 3):
            spread_copy(n, buffer, k).wait_send()
            back_copy(n, k).wait_send()

    column = lax.broadcasted_iota(jnp.int32, (ROWS, PAD), 1)
    first_half = column % HEAD < HEAD // 2

    def turn(block, sign):
        ahead = pltpu.roll(block, PAD - HEAD // 2, 1)
        behind = pltpu.roll(block, HEAD // 2, 1)
        return jnp.where(first_half, -sign * ahead, sign * behind)

    def rotated(block):
        return block * cosine[...] + turn(block, 1.0) * sine[...]

    def rotated_back(block):
        return block * cosine[...] + turn(block * sine[...], -1.0)

    def inverse_rms(x):
        return lax.rsqrt(jnp.mean(x * x, axis=-1, keepdims=True) + norm_eps)

    def head_lanes(h):
        return slice(h * HEAD, (h + 1) * HEAD)

    def soft_weights(l, kv):
        rows = jnp.concatenate([qrot[l, :, head_lanes(kv * SHARE + i)] for i in range(SHARE)], axis=0)
        keys = krot[l, :, head_lanes(kv)]
        scores = dot_t(rows, keys) * score_scale
        scores = scores + jnp.concatenate([bias[...]] * SHARE, axis=0)
        weights = jnp.exp(scores - jnp.max(scores, axis=-1, keepdims=True))
        return rows, keys, weights / jnp.sum(weights, axis=-1, keepdims=True)

    def attention_forward(l):
        x = stream[l]
        normed = (x * inverse_rms(x) * gain_full[l : l + 1, :]).astype(BF)
        npad[l] = dot(normed, place[...]).astype(BF)

        def project(weights, width):
            total = jnp.zeros((ROWS, width), F32)
            for g in range(8):
                total = total + dot(npad[l, :, g * PAD : g * PAD + SHARD], weights[l, g // 2, g % 2])
            return total

        gather_end(l, (0, 1, 2))
        wide[:, :D] = project(fq, D)
        narrow[:, :KV] = project(fk, KV)
        vals[l, :, :KV] = project(fv, KV).astype(BF)
        for j in range(8):
            at = slice(j * PAD, (j + 1) * PAD)
            qrot[l, :, at] = rotated(wide[:, at]).astype(BF)
        for j in range(3):
            at = slice(j * PAD, (j + 1) * PAD)
            krot[l, :, at] = rotated(narrow[:, at]).astype(BF)
        for kv in range(KV_HEADS):
            rows, keys, soft = soft_weights(l, kv)
            out = dot(soft.astype(BF), vals[l, :, head_lanes(kv)]).astype(BF)
            for i in range(SHARE):
                mixed[:, head_lanes(kv * SHARE + i)] = out[i * ROWS : (i + 1) * ROWS]
        mpad[l] = dot(mixed[:, :D], place[...]).astype(BF)
        gather_end(l, (3,))
        total = x
        for g in range(8):
            total = total + dot(mpad[l, :, g * PAD : g * PAD + SHARD], fo[l, g // 2, g % 2])
        hidden[l] = total
        acts_in[l, y] = (total * inverse_rms(total) * gain_full[2 + l : 3 + l, :]).astype(BF)

    def mlp_forward(l, n):
        buffer = acts_in.at[l]

        def block(i, carry):
            k = order(i)
            b = (y - k + 4) % 4

            @pl.when(i > 0)
            def _():
                arrived(n, buffer, k)

            rows = acts_in[l, b]
            total = jnp.zeros((ROWS, D), F32)
            for p in range(2):
                gate = dot(rows, fg[l, p])
                up = dot(rows, fu[l, p])
                act = (gate * jax.nn.sigmoid(gate) * up).astype(BF)
                s_gate[l, p, b] = gate.astype(BF)
                s_up[l, p, b] = up.astype(BF)
                s_act[l, p, b] = act
                total = total + dot(act, fd[l, p])

            @pl.when(i == 0)
            def _():
                own_part[...] = total

            @pl.when(i > 0)
            def _():
                parts[n % 2, k - 1] = total.astype(BF)
                back_copy(n, k).start()

            return carry

        lax.fori_loop(0, 4, block, 0)

    def mlp_backward(l, n):
        buffer = grads_in.at[1 - l]

        def block(i, carry):
            k = order(i)
            b = (y - k + 4) % 4

            @pl.when(i > 0)
            def _():
                arrived(n, buffer, k)

            rows = grads_in[1 - l, b]
            total = jnp.zeros((ROWS, D), F32)
            for p in range(2):
                grad_active = dot_t(rows, fd[l, p])
                gate = s_gate[l, p, b].astype(F32)
                up = s_up[l, p, b].astype(F32)
                sig = jax.nn.sigmoid(gate)
                grad_gate = (grad_active * up * sig * (1.0 + gate * (1.0 - sig))).astype(BF)
                grad_up = (grad_active * gate * sig).astype(BF)
                s_gg[p, b] = grad_gate
                s_gu[p, b] = grad_up
                total = total + dot_t(grad_gate, fg[l, p]) + dot_t(grad_up, fu[l, p])

            @pl.when(i == 0)
            def _():
                own_part[...] = total

            @pl.when(i > 0)
            def _():
                parts[n % 2, k - 1] = total.astype(BF)
                back_copy(n, k).start()

            return carry

        lax.fori_loop(0, 4, block, 0)

        if l == 0:
            for copy in out_pairs(1):
                copy.wait()

        def grads(p, carry):
            ins = acts_in[l].reshape(4 * ROWS, D)
            tg[p] = t_dot(ins, s_gg[p].reshape(4 * ROWS, FFS)).astype(BF)
            tu[p] = t_dot(ins, s_gu[p].reshape(4 * ROWS, FFS)).astype(BF)
            td[p] = t_dot(
                s_act[l, p].reshape(4 * ROWS, FFS), grads_in[1 - l].reshape(4 * ROWS, D)
            ).astype(BF)
            return carry

        lax.fori_loop(0, 2, grads, 0)
        for copy in out_pairs(l):
            copy.start()

    def out_pairs(l):
        return [
            pltpu.make_async_copy(src, dst.at[l], local.at[17 + l * 3 + a])
            for a, (src, dst) in enumerate(((tg, gg), (tu, gu), (td, gd)))
        ]

    def slab_loop(body):
        def run(g, carry):
            body(g, g // 2, g % 2)
            return carry

        lax.fori_loop(0, 8, run, 0)

    def norm_back(x, grad_normed, gain_row):
        r = inverse_rms(x)
        u = grad_normed * gain_row
        back = r * u - x * (r * r * r) * jnp.mean(u * x, axis=-1, keepdims=True)
        return back, jnp.sum(grad_normed * x * r, axis=0, keepdims=True)

    def attention_backward(l, n):
        grad_input = collect(n, own_part[...])
        back, grad_gain_two = norm_back(hidden[l], grad_input, gain_full[2 + l : 3 + l, :])
        grad_hidden = grad[...] + back
        grad[...] = grad_hidden
        grad_low = grad_hidden.astype(BF)
        glow[...] = grad_low

        def back_out(g, h, i):
            wide_pad[:, lanes(g, SHARD)] = dot_t(glow[...], fo[l, h, i])

        slab_loop(back_out)
        gmix[...] = dot_t(wide_pad[...].astype(BF), place[...]).astype(BF)

        def grads_out(g, h, i):
            go[l, h, i] = t_dot(mpad[l, :, lanes(g, PAD)], glow[...]).astype(BF)

        slab_loop(grads_out)
        for kv in range(KV_HEADS):
            rows, keys, soft = soft_weights(l, kv)
            heads = [kv * SHARE + i for i in range(SHARE)]
            gm = jnp.concatenate([gmix[:, head_lanes(h)] for h in heads], axis=0)
            grad_probs = dot_t(gm, vals[l, :, head_lanes(kv)])
            inner = jnp.sum(soft * grad_probs, axis=-1, keepdims=True)
            grad_scores = (soft * (grad_probs - inner)).astype(BF)
            grad_rows = dot(grad_scores, keys) * score_scale
            for i, h in enumerate(heads):
                wide[:, head_lanes(h)] = grad_rows[i * ROWS : (i + 1) * ROWS]
            narrow[:, head_lanes(kv)] = t_dot(grad_scores, rows) * score_scale
            gproj_v[:, head_lanes(kv)] = t_dot(soft.astype(BF), gm).astype(BF)
        for j in range(8):
            at = slice(j * PAD, (j + 1) * PAD)
            gproj_q[:, at] = rotated_back(wide[:, at]).astype(BF)
        for j in range(3):
            at = slice(j * PAD, (j + 1) * PAD)
            gproj_k[:, at] = rotated_back(narrow[:, at]).astype(BF)

        def back_in(g, h, i):
            wide_pad[:, lanes(g, SHARD)] = (
                dot_t(gproj_q[:, :D], fq[l, h, i])
                + dot_t(gproj_k[:, :KV], fk[l, h, i])
                + dot_t(gproj_v[:, :KV], fv[l, h, i])
            )

        slab_loop(back_in)
        high, low = halves(wide_pad[...])
        grad_normed = dot_t(high, place[...]) + dot_t(low, place[...])
        back, grad_gain_one = norm_back(stream[l], grad_normed, gain_full[l : l + 1, :])
        grad_stream = grad[...] + back
        grad[...] = grad_stream
        if l > 0:
            grads_in[1, y] = grad_stream.astype(BF)
            spread(3, grads_in.at[1])
        else:
            out_grad[...] = grad_stream
        row = lax.broadcasted_iota(jnp.int32, (16, D), 0)
        both = jnp.where(row == 0, grad_gain_one, 0.0) + jnp.where(row == 1, grad_gain_two, 0.0)
        high, low = halves(both)
        gain_grad[...] = dot(high, place[...]) + dot(low, place[...])

        def grads_in_proj(g, h, i):
            left = npad[l, :, lanes(g, PAD)]
            total = t_dot(left, gproj_q[:, :D])
            rows = lax.broadcasted_iota(jnp.int32, (PAD, PAD), 0)
            one = gain_grad[0:1, lanes(g, PAD)]
            two = gain_grad[1:2, lanes(g, PAD)]
            corner = (
                total[:, :PAD]
                + jnp.where(rows == SHARD, one, 0.0)
                + jnp.where(rows == SHARD + 1, two, 0.0)
            )
            gq[l, h, i] = total.astype(BF)
            gq[l, h, i, :, :PAD] = corner.astype(BF)
            gk[l, h, i] = t_dot(left, gproj_k[:, :KV]).astype(BF)
            gv[l, h, i] = t_dot(left, gproj_v[:, :KV]).astype(BF)

        slab_loop(grads_in_proj)

    gather_begin(0, range(4))
    gain_keep.start()
    for copy in gain_send.values():
        copy.start()
    wide_column = lax.broadcasted_iota(jnp.int32, (D, 8 * PAD), 1)
    row = lax.broadcasted_iota(jnp.int32, (D, 8 * PAD), 0)
    lane = wide_column % PAD
    place[...] = jnp.where(
        jnp.logical_and(lane < SHARD, (wide_column // PAD) * SHARD + lane == row), 1.0, 0.0
    ).astype(BF)
    wide[...] = jnp.zeros_like(wide)
    wide_pad[...] = jnp.zeros_like(wide_pad)
    narrow[...] = jnp.zeros_like(narrow)
    stream[0] = tokens[...].astype(F32)
    gather_pass(0, (0, 1, 2))
    pairs_begin(0)
    gather_pass(0, (3,))
    gather_begin(1, range(4))
    pairs_begin(1)
    gain_keep.wait()
    for copy in gain_send.values():
        copy.wait()
    for g in range(8):
        gain_pad[:, g * PAD : (g + 1) * PAD] = fgain[g // 2, g % 2]
    gain_full[...] = dot_t(gain_pad[...], place[...])
    attention_forward(0)
    spread(0, acts_in.at[0])
    gather_pass(1, range(4))
    pairs_pass(0)
    pairs_pass(1)
    pairs_end(0)
    mlp_forward(0, 0)
    grads_in[0, y] = cotangent[...]
    grad[...] = cotangent[...].astype(F32)
    stream[1] = collect(0, own_part[...] + hidden[0])
    spread(2, grads_in.at[0])
    attention_forward(1)
    spread(1, acts_in.at[1])
    pairs_end(1)
    sent(0, acts_in.at[0])
    mlp_forward(1, 1)
    result = own_part[...] + hidden[1]
    wide[:, :D] = result
    mlp_backward(1, 2)
    out_act[...] = collect(1, wide[:, :D]).astype(BF)
    attention_backward(1, 2)
    sent(1, acts_in.at[1])
    mlp_backward(0, 3)
    attention_backward(0, 3)
    for copy in out_pairs(0):
        copy.wait()
    sent(2, grads_in.at[0])
    sent(3, grads_in.at[1])
    for l in range(LAYERS):
        gather_sent(l, range(4))
        for a in range(3):
            cross_m[l, a].wait_send()
            pass_m[l, a].wait_send()


def step(tokens, cotangent, cosine, sine, bias, gains, *weights):
    L = LAYERS

    def buf(*shape, dtype=BF):
        return pltpu.VMEM(shape, dtype)

    def out(*shape, dtype=BF):
        return jax.ShapeDtypeStruct(shape, dtype)

    count = 160
    return pl.pallas_call(
        step_kernel,
        out_shape=(
            out(ROWS, D),
            out(ROWS, D, dtype=F32),
            out(L, 4, 2, PAD, D),
            out(L, 4, 2, PAD, KV),
            out(L, 4, 2, PAD, KV),
            out(L, 4, 2, PAD, D),
            out(L, 2, D, FFS),
            out(L, 2, D, FFS),
            out(L, 2, FFS, D),
        ),
        in_specs=[VMEM] * 6 + [ANY] * 7,
        out_specs=[VMEM] * 6 + [ANY] * 3,
        scratch_shapes=[
            buf(L, 4, 2, SHARD, D),
            buf(L, 4, 2, SHARD, KV),
            buf(L, 4, 2, SHARD, KV),
            buf(L, 4, 2, SHARD, D),
            buf(L, 2, D, FFS),
            buf(L, 2, D, FFS),
            buf(L, 2, FFS, D),
            buf(4, 2, 16, PAD),
            buf(D, 8 * PAD),
            buf(16, D, dtype=F32),
            buf(16, 8 * PAD),
            buf(L, ROWS, D, dtype=F32),
            buf(L, ROWS, D, dtype=F32),
            buf(ROWS, D, dtype=F32),
            buf(ROWS, 8 * PAD, dtype=F32),
            buf(ROWS, 3 * PAD, dtype=F32),
            buf(ROWS, 8 * PAD, dtype=F32),
            buf(L, ROWS, 8 * PAD),
            buf(L, ROWS, 8 * PAD),
            buf(L, ROWS, 8 * PAD),
            buf(L, ROWS, 3 * PAD),
            buf(L, ROWS, 3 * PAD),
            buf(ROWS, 8 * PAD),
            buf(ROWS, 8 * PAD),
            buf(ROWS, 3 * PAD),
            buf(ROWS, 3 * PAD),
            buf(ROWS, D),
            buf(L, 4, ROWS, D),
            buf(2, 4, ROWS, D),
            buf(2, 3, ROWS, D),
            buf(2, 3, ROWS, D),
            buf(L, 2, 4, ROWS, FFS),
            buf(L, 2, 4, ROWS, FFS),
            buf(L, 2, 4, ROWS, FFS),
            buf(2, 4, ROWS, FFS),
            buf(2, 4, ROWS, FFS),
            buf(2, D, FFS),
            buf(2, D, FFS),
            buf(2, FFS, D),
            buf(ROWS, D, dtype=F32),
            buf(ROWS, D),
            buf(16, 8 * PAD, dtype=F32),
            pltpu.SemaphoreType.DMA((count,)),
            pltpu.SemaphoreType.DMA((count,)),
            pltpu.SemaphoreType.DMA((24,)),
        ],
        compiler_params=pltpu.CompilerParams(
            collective_id=1, has_side_effects=True, vmem_limit_bytes=63 * 2**20
        ),
    )(tokens, cotangent, cosine, sine, bias, gains, *weights)


def add_into(dst, others, step=16):
    rows = dst.shape[0]

    def body(i, carry):
        at = pl.ds(pl.multiple_of(i * step, step), step)
        total = dst[at, :].astype(F32)
        for other in others:
            total = total + other[at, :].astype(F32)
        dst[at, :] = total.astype(dst.dtype)
        return carry

    lax.fori_loop(0, rows // step, body, 0)


def add_to(dst, terms, step=16):
    rows = dst.shape[0]

    def body(i, carry):
        at = pl.ds(pl.multiple_of(i * step, step), step)
        total = terms[0][at, :].astype(F32)
        for other in terms[1:]:
            total = total + other[at, :].astype(F32)
        dst[at, :] = total.astype(dst.dtype)
        return carry

    lax.fori_loop(0, rows // step, body, 0)


SLABS = (D, KV, KV, D)
PAIRS = ((D, FFS), (D, FFS), (FFS, D))


def reduce_kernel(*refs):
    def take(count):
        nonlocal refs
        got, refs = refs[:count], refs[count:]
        return got

    gs, gp = take(4), take(3)
    fs, fp = take(4), take(3)
    ss, sp = take(4), take(3)
    xs, xp = take(4), take(3)
    ys, ls = take(4), take(4)
    zs, zp = take(4), take(3)
    ps, pp = take(4), take(3)
    hs, hp = take(4), take(3)
    send, recv = refs
    x_hi, z, core, y, x_lo = coords()
    sems = (send, recv)
    sibling = device(x_hi, z, 1 - core, y, x_lo)
    near = [device(x_hi, z, core, y, 1 - x_lo), device(1 - x_hi, z, core, y, 1 - x_lo)]
    far = device(1 - x_hi, z, core, y, x_lo)
    ring_y = {k: device(x_hi, z, core, (y + k) % 4, x_lo) for k in (1, 2, 3)}
    ring_z = {k: device(x_hi, (z + k) % 4, core, y, x_lo) for k in (1, 2, 3)}
    greet(list(ring_y.values()) + list(ring_z.values()) + near + [far, sibling])
    home = core == x_lo
    slots = Slots()
    layers = (1, 0)

    def part(rows, where):
        return pl.ds(pl.multiple_of(where * (rows // 4), 16), rows // 4)

    pieces = [(sp[a], zp[a], pp[a], hp[a], fp[a], PAIRS[a][0]) for a in range(3)] + [
        (ls[a], zs[a], ps[a], hs[a], fs[a], PAD) for a in range(4)
    ]
    pair, over_x, over_y, over_z, over_h, out_z, last = {}, {}, {}, {}, {}, {}, {}
    for l in layers:
        for a in range(7):
            if a < 3:
                own, got = gp[a].at[l, 1 - core], sp[a].at[l]
                src, dst = sp[a].at[l], xp[a].at[l]
            else:
                own, got = gs[a - 3].at[l, :, 1 - core], ss[a - 3].at[l]
                src, dst = ss[a - 3].at[l], xs[a - 3].at[l]
                for k in (1, 2, 3):
                    over_y[l, a, k] = remote(
                        src.at[(y + k) % 4], ys[a - 3].at[l, k - 1], sems, slots.take(), ring_y[k]
                    )
            pair[l, a] = remote(own, got, sems, slots.take(), sibling)
            over_x[l, a] = remote(src, dst, sems, slots.take(), near[l])
            src, zb, pb, hb, fb, rows = pieces[a]
            for k in (1, 2, 3):
                over_z[l, a, k] = remote(
                    src.at[l, part(rows, (z + k) % 4)], zb.at[l, k - 1], sems, slots.take(), ring_z[k]
                )
                mine = fb.at[l, part(rows, z)]
                out_z[l, a, k] = remote(mine, mine, sems, slots.take(), ring_z[k])
            over_h[l, a] = remote(pb.at[l], hb.at[l], sems, slots.take(), far)
            last[l, a] = remote(fb.at[l], fb.at[l], sems, slots.take(), sibling)
    for l in layers:
        for a in range(7):
            pair[l, a].start()
    for l in layers:
        for a in range(7):
            pair[l, a].wait_recv()
            if a < 3:
                add_into(sp[a].at[l], [gp[a].at[l, core]])
            else:
                for q in range(4):
                    add_into(ss[a - 3].at[l, q], [gs[a - 3].at[l, q, core]])

            @pl.when(jnp.logical_not(home))
            def _():
                over_x[l, a].start()

    @pl.when(home)
    def _():
        for l in layers:
            for a in range(7):
                over_x[l, a].wait_recv()
                if a < 3:
                    add_into(sp[a].at[l], [xp[a].at[l]])
                    for k in (1, 3, 2):
                        over_z[l, a, k].start()
                else:
                    for k in (1, 3, 2, 0):
                        q = (y + k) % 4
                        add_into(ss[a - 3].at[l, q], [xs[a - 3].at[l, q]])
                        if k:
                            over_y[l, a, k].start()
        for l in layers:
            for a in range(3, 7):
                for k in (1, 3, 2):
                    over_y[l, a, k].wait_recv()
                add_to(ls[a - 3].at[l], [ss[a - 3].at[l, y]] + [ys[a - 3].at[l, j] for j in range(3)])
                for k in (1, 3, 2):
                    over_z[l, a, k].start()
        for l in layers:
            for a in range(7):
                src, zb, pb, hb, fb, rows = pieces[a]
                for k in (1, 3, 2):
                    over_z[l, a, k].wait_recv()
                add_to(pb.at[l], [src.at[l, part(rows, z)]] + [zb.at[l, j] for j in range(3)])
                over_h[l, a].start()
        for l in layers:
            for a in range(7):
                src, zb, pb, hb, fb, rows = pieces[a]
                over_h[l, a].wait_recv()
                add_to(fb.at[l, part(rows, z)], [pb.at[l], hb.at[l]])
                for k in (1, 3, 2):
                    out_z[l, a, k].start()
        for l in layers:
            for a in range(7):
                for k in (1, 3, 2):
                    out_z[l, a, k].wait_recv()
                last[l, a].start()
        for l in layers:
            for a in range(7):
                last[l, a].wait_send()
                over_h[l, a].wait_send()
                for k in (1, 3, 2):
                    over_z[l, a, k].wait_send()
                    out_z[l, a, k].wait_send()
                    if a >= 3:
                        over_y[l, a, k].wait_send()

    @pl.when(jnp.logical_not(home))
    def _():
        for copy in over_x.values():
            copy.wait_send()
        for copy in last.values():
            copy.wait_recv()

    for copy in pair.values():
        copy.wait_send()


def reduce(*grads):
    count = 180
    L = LAYERS

    def bufs(slab, pair_of):
        return [pltpu.VMEM(slab + (n,), BF) for n in SLABS] + [
            pltpu.VMEM(pair_of(r) + (n,), BF) for r, n in PAIRS
        ]

    full = bufs((L, 4, PAD), lambda r: (L, r))
    quarter = bufs((L, PAD // 4), lambda r: (L, r // 4))
    return pl.pallas_call(
        reduce_kernel,
        out_shape=[jax.ShapeDtypeStruct((L, PAD, n), BF) for n in SLABS]
        + [jax.ShapeDtypeStruct((L, r, n), BF) for r, n in PAIRS],
        in_specs=[VMEM] * 7,
        out_specs=[VMEM] * 7,
        scratch_shapes=full
        + full
        + bufs((L, 3, PAD), lambda r: (L, 3, r))[:4]
        + bufs((L, PAD), lambda r: (L, r))[:4]
        + bufs((L, 3, PAD // 4), lambda r: (L, 3, r // 4))
        + quarter
        + quarter
        + [pltpu.SemaphoreType.DMA((count,)), pltpu.SemaphoreType.DMA((count,))],
        compiler_params=pltpu.CompilerParams(
            collective_id=2, has_side_effects=True, vmem_limit_bytes=63 * 2**20
        ),
    )(*grads)


def rope_tables(positions):
    steps_half = jnp.arange(HEAD // 2, dtype=jnp.float32)
    inverse = rope_base ** (-2.0 * steps_half / HEAD)
    angles = positions[:, None] * inverse[None, :]
    cosine = jnp.cos(angles)
    sine_table = jnp.sin(angles)
    return (
        jnp.concatenate([cosine, cosine], axis=1),
        jnp.concatenate([sine_table, sine_table], axis=1),
    )


def layout(seq_lengths, amount):
    finish = jnp.cumsum(seq_lengths)
    indices = jnp.arange(amount, dtype=jnp.int32)
    documents = jnp.sum((indices[:, None] >= finish[None, :]).astype(jnp.int32), axis=1)
    starts = finish - seq_lengths
    member = documents[:, None] == jnp.arange(seq_lengths.shape[0], dtype=jnp.int32)[None, :]
    begins = jnp.sum(jnp.where(member, starts[None, :], 0), axis=1)
    return (documents, indices - begins)


def shards(
    tokens, cotangent, lengths, gain_attn, w_query, w_key, w_value, w_out, gain_mlp, w_gate, w_up, w_down
):
    doc_own, pos_own = layout(lengths[0], ROWS)
    cosine, sine_table = rope_tables(pos_own.astype(F32))
    row_index = jnp.arange(ROWS, dtype=jnp.int32)
    allowed = (doc_own[:, None] == doc_own[None, :]) & (row_index[None, :] <= row_index[:, None])
    bias = jnp.where(allowed, 0.0, masked_value).astype(F32)
    twice = functools.partial(jnp.tile, reps=(1, 2))
    gains = jnp.pad(jnp.concatenate([gain_attn, gain_mlp], axis=0), ((0, 12), (0, PAD - SHARD)))
    act, grad, *grads = step(
        tokens, cotangent, twice(cosine), twice(sine_table), bias, gains,
        w_query, w_key, w_value, w_out, w_gate, w_up, w_down,
    )
    rq, rk, rv, ro, rg, ru, rd = (a.astype(F32) for a in reduce(*grads))
    return (
        act,
        grad,
        rq[:, SHARD, :SHARD],
        rq[:, :SHARD],
        rk[:, :SHARD],
        rv[:, :SHARD],
        ro[:, :SHARD],
        rq[:, SHARD + 1, :SHARD],
        rg,
        ru,
        rd,
    )


def solution(mesh):
    in_specs = (
        P(("replica", "group"), None),
        P(("replica", "group"), None),
        P(("replica", "group"), None),
        P(None, "group"),
        P(None, "group", None),
        P(None, "group", None),
        P(None, "group", None),
        P(None, "group", None),
        P(None, "group"),
        P(None, None, "group"),
        P(None, None, "group"),
        P(None, "group", None),
    )
    out_specs = (
        P(("replica", "group"), None),
        P(("replica", "group"), None),
        P(None, "group"),
        P(None, "group", None),
        P(None, "group", None),
        P(None, "group", None),
        P(None, "group", None),
        P(None, "group"),
        P(None, None, "group"),
        P(None, None, "group"),
        P(None, "group", None),
    )
    return jax.shard_map(shards, mesh=mesh, in_specs=in_specs, out_specs=out_specs, check_vma=False)
```

time: 2280 us -> 386 us (0.17)
  waiting for transfers between devices: 1720 us -> 0 us
  Pallas kernels: 0 us -> 348 us
  blocking collectives: 281 us -> 0 us
  matrix products: 176 us -> 0 us
  other arithmetic: 33.2 us -> 8.75 us
    reduce_scatter x10 -> x0, waiting for transfers between devices: 875 us -> none  [the longest x2 224 us: shards(): lax.psum_scatter(grad_up_w.astype(jnp.bfloat16), 'group', scatter_dimensi...]
    all_gather x10 -> x0, waiting for transfers between devices: 668 us -> none  [the longest x2 215 us: fetch_mlp(): lax.all_gather(w_up[layer_index], 'group', axis=1, tiled=True)]
    pallas_call x0 -> x2, Pallas kernels: none -> 348 us  [the longest x1 202 us: step(): pl.pallas_call(step_kernel, out_shape=(out(ROWS, D), out(ROWS, D, dtype=F...]
    all_gather x4 -> x0, blocking collectives: 211 us -> none  [the longest x2 116 us: fetch_attention(): lax.all_gather(w_value[layer_index], 'group', axis=0, tiled=True)]
    dot_general x112 -> x0, matrix products: 176 us -> none  [the longest x14 41.4 us: transposed_times(): lax.dot_general(left_side, right_side, (((0,), (0,)), ((), ())), preferre...]
    psum x1 -> x0, waiting for transfers between devices: 93.6 us -> none  [shards(): lax.psum(stacked[1].astype(jnp.bfloat16), 'replica').astype(jnp.float32)]
    unnamed x23 -> x0, waiting for transfers between devices: 88.4 us -> none
    psum x1 -> x0, blocking collectives: 37 us -> none  [shards(): lax.psum(stacked[0].astype(jnp.bfloat16), 'replica').astype(jnp.float32)]
  transfers between devices with their start and end apart: 22 -> 0, of which waited for: 20 -> 0; matrix products, arithmetic and copies ran while one was open for 6% -> 0% of each run, Pallas kernels for 0% -> 0%
where the time goes in v2:
time: 386 us; the launch traced here: 380 us
  Pallas kernels  348 us (90%)
  local copies, waits for them, and re-layouts  22.5 us (6%)
  other arithmetic  8.75 us (2%)
    pallas_call x1, Pallas kernels, step(): pl.pallas_call(step_kernel, out_shape=(out(ROWS, D), out(ROWS, D, dtype=F...  202 us
    pallas_call x1, Pallas kernels, reduce(): pl.pallas_call(reduce_kernel, out_shape=[jax.ShapeDtypeStruct((L, PAD, n)...  145 us
    unnamed x28, local copies, waits for them, and re-layouts  18.6 us

profile of v2, /device:TPU:1, one launch (start us, length us, event | category | flops | bytes accessed | tf_op | source)
XLA Modules:
  0.0 380.1 jit_solution(5764748496741207553)
XLA Ops:
  0.7 1.0 reduce-window.4
  1.6 0.1 convert_reduce_fusion
  1.7 0.7 fusion.8
  2.4 0.1 select_reduce_fusion
  2.5 1.3 fusion.7.gains
  3.7 0.1 multiply_sine_fusion
  3.9 0.7 copy.51.cosine
  4.7 0.7 fusion.1.bias
  5.4 0.7 copy.52.sine
  6.1 1.7 copy.53.wk
  7.8 1.7 copy.54.wv
  9.5 1.8 copy.49.tokens
  11.3 0.8 copy.50.cotangent
  12.2 0.0 copy-done.3
  12.2 1.6 copy.55.wg
  13.7 1.6 copy.56.wu
  15.3 202.4 %shard_map.203 = (bf16[128,960]{1,0:T(8,128)(2,1)}, f32[128,960]{1,0:T(8,128)}, bf16[2,4,2,128,960]{4,3,2,1,0:T(8,128)(2,1)}, bf16[2,4,2,128,320]{4,3,2,1,0:T(8,...) custom-call(bf16[128,960]{1,0:T(8,128)(2,1)} %copy.49.tokens, ...), custom_call_target="tpu_custom_call" | custom-call | tf_op jit(solution)/shard_map/pallas_call | solution.py:570
  217.7 1.8 copy.57
  219.5 2.0 copy.58
  221.6 145.5 %shard_map.204 = (bf16[2,128,960]{2,1,0:T(8,128)(2,1)}, bf16[2,128,320]{2,1,0:T(8,128)(2,1)}, bf16[2,128,320]{2,1,0:T(8,128)(2,1)}, bf16[2,128,960]{2,1,0:T(8,12...) custom-call(bf16[2,4,2,128,960]{4,3,2,1,0:T(8,128)(2,1)} %get-tuple-element.29.ref, ...), custom_call_target="tpu_custom_call" | custom-call | tf_op jit(solution)/shard_map/pallas_call | solution.py:816
  367.0 1.4 fusion.9
  368.4 0.9 slice_convert_fusion.2
  369.4 0.9 copy.59
  370.3 1.0 slice_convert_fusion.1
  371.3 0.9 copy.60
  372.2 0.0 copy-done
  372.2 1.1 slice.37
  373.2 0.0 copy-done.6
  373.2 1.0 slice_convert_fusion
  374.3 1.9 copy.61
  376.2 1.9 copy.62
  378.1 1.8 convert_element_type.32
  (18 shorter events, 0.1 us)
Async XLA Ops:
  0.6 11.5 %copy-start.3 = (bf16[2,960,320]{1,2,0:T(8,128)(2,1)S(1)}, bf16[2,960,320]{1,2,0:T(8,128)(2,1)}, u32[]{:S(2)}) copy-start(bf16[2,960,320]{1,2,0:T(8,128)(2,1)} %param.21) | copy-start | bytes 3686404
  0.7 10.7 %copy-start.7 = (bf16[128,960]{0,1:T(8,128)(2,1)S(1)}, bf16[128,960]{0,1:T(8,128)(2,1)}, u32[]{:S(2)}) copy-start(bf16[128,960]{0,1:T(8,128)(2,1)} %param.13) | copy-start | bytes 737284
  11.3 2.4 copy-start.4
  367.0 5.1 %copy-start = (bf16[2,128,960]{2,1,0:T(8,128)(2,1)S(1)}, bf16[2,128,960]{2,1,0:T(8,128)(2,1)}, u32[]{:S(2)}) copy-start(bf16[2,128,960]{2,1,0:T(8,128)(2,1)} %get-tuple-element.36) | copy-start | bytes 1474564
  370.3 3.0 copy-start.6
  372.2 2.1 copy-start.2
  374.3 1.9 copy-start.1
  376.2 1.9 copy-start.5
